TPU v7x, 128 devices: a whole 4x4x4 slice. The times are simulated.
128 devices in a mesh: event: 4 (over x), region: 32 (over z, y, core).
Axes of the slice: x: 4, y: 4, z: 4, core: 2. Of those that a mesh axis runs over, the one named last changes fastest.
Arguments:
- queries_in: bfloat16 [4096, 512], P('event'), parts along dimension 0, may hold values from -144 to 144
- hits_in: bfloat16 [131072, 512], P(('event', 'region')), parts along dimension 0, may hold values from -6 to 6
- w_query: bfloat16 [512, 512], replicated, may hold values from -0.25 to 0.25
- w_key: bfloat16 [512, 512], replicated, may hold values from -0.25 to 0.25
- w_value: bfloat16 [512, 512], replicated, may hold values from -0.25 to 0.25
- w_out: bfloat16 [512, 512], replicated, may hold values from -0.25 to 0.25
- mask_list: int32 [32, 64], P('event'), parts along dimension 0, may hold values from 0 to 255, all different within a row
- grad_out: bfloat16 [4096, 512], P('event'), parts along dimension 0, may hold values from -6 to 6
Outputs:
- layer_out: bfloat16 [4096, 512], P('event'), parts along dimension 0
- grad_queries: bfloat16 [4096, 512], P('event'), parts along dimension 0
- grad_hits: bfloat16 [131072, 512], P(('event', 'region')), parts along dimension 0
- grad_wq: float32 [2048, 512], P('event'), parts along dimension 0
- grad_wk: float32 [2048, 512], P('event'), parts along dimension 0
- grad_wv: float32 [2048, 512], P('event'), parts along dimension 0
- grad_wo: float32 [2048, 512], P('event'), parts along dimension 0
There are 4 independent parts, one for each index of `event`. A program takes and returns all parts, laid end to end along the dimension named above; an argument that names none is the same for every part. Nothing has to cross between parts.
Inputs may be any that keep to these rules, and one draw needn't show every extreme that they name: `mask_list`: each row names 64 different hit blocks, and every hit block is named by some row.
All inputs are finite; a program needn't handle non-finite values.
Results may differ from a plain program's by a relative error of at most 0.04.
The roundings to bfloat16 on the way count: a program that leaves them out, or rounds other values in their place, can miss the bound.
Values may be sent and summed in bfloat16 or wider, within the bound.
A program may use at most 192 MiB of HBM per device.

v0:
```python
import math

import jax
import jax.numpy as jnp
from jax import lax
from jax.sharding import PartitionSpec as P

HEADS = 8
BLOCK = 128
ROWS = 512


def merged(shard, axis, combine):
    everything = jax.tree.map(lambda part: lax.all_gather(part, axis), shard)
    initial = jax.tree.map(lambda part: part[0], everything)

    def lap(k, so_far):
        return combine(so_far, jax.tree.map(lambda part: part[k], everything))

    return lax.fori_loop(1, lax.axis_size(axis), lap, initial)


def split_heads(array):
    return array.reshape(array.shape[:-1] + (HEADS, array.shape[-1] // HEADS))


def merge_partials(first, second):
    numer_a, max_a, total_a = first
    numer_b, max_b, total_b = second
    peak = jnp.maximum(max_a, max_b)
    scale_a = jnp.exp(max_a - peak)
    scale_b = jnp.exp(max_b - peak)
    head_dim = numer_a.shape[-1] // max_a.shape[-1]
    numer = numer_a * jnp.repeat(scale_a, head_dim, axis=-1) + numer_b * jnp.repeat(
        scale_b, head_dim, axis=-1
    )
    return (numer, peak, total_a * scale_a + total_b * scale_b)


def on_device(queries_in, hits_in, w_query, w_key, w_value, w_out, mask_list, grad_out):
    f32 = jnp.float32
    bf16 = jnp.bfloat16
    regions = lax.axis_size("region")
    region_index = lax.axis_index("region")
    n_queries, width = queries_in.shape
    n_hits = hits_in.shape[0]
    head_dim = width // HEADS
    score_scale = 1.0 / math.sqrt(head_dim)
    hit_blocks = n_hits // BLOCK
    all_blocks = hit_blocks * regions
    groups = n_queries // ROWS
    blockmask = jnp.any(
        mask_list[:, :, None] == jnp.arange(all_blocks, dtype=jnp.int32)[None, None, :], axis=1
    )
    local_blocks = lax.dynamic_slice_in_dim(blockmask, region_index * hit_blocks, hit_blocks, 1)
    column_mask = jnp.repeat(local_blocks, BLOCK, axis=1)
    column_groups = column_mask.reshape(groups, ROWS // BLOCK, n_hits)
    query = jnp.dot(queries_in, w_query, preferred_element_type=f32).astype(bf16)
    keys = jnp.dot(hits_in, w_key, preferred_element_type=f32).astype(bf16)
    vals = jnp.dot(hits_in, w_value, preferred_element_type=f32).astype(bf16)
    key_heads = split_heads(keys)
    value_heads = split_heads(vals)
    query_groups = query.reshape(groups, ROWS, width)

    def group_scores(query_rows, block_rows):
        allowed = jnp.repeat(block_rows, BLOCK, axis=0)[:, None, :]
        scores = (
            jnp.einsum(
                "rhd,khd->rhk", split_heads(query_rows), key_heads, preferred_element_type=f32
            )
            * score_scale
        )
        return (allowed, scores)

    def forward_group(inputs):
        query_rows, block_rows = inputs
        allowed, scores = group_scores(query_rows, block_rows)
        masked = jnp.where(allowed, scores, -1e30)
        maxima = jnp.max(masked, axis=2)
        exponents = jnp.where(allowed, jnp.exp(masked - maxima[..., None]), 0.0)
        totals = jnp.sum(exponents, axis=2)
        numer = jnp.einsum(
            "rhk,khd->rhd", exponents.astype(bf16), value_heads, preferred_element_type=f32
        )
        return (numer.reshape(ROWS, width), maxima, totals)

    numer_parts, maxima_parts, totals_parts = lax.map(forward_group, (query_groups, column_groups))
    numer_local = numer_parts.reshape(n_queries, width)
    maxima_local = maxima_parts.reshape(n_queries, HEADS)
    totals_local = totals_parts.reshape(n_queries, HEADS)
    numer, peak, total = merged((numer_local, maxima_local, totals_local), "region", merge_partials)
    attended = (numer / jnp.repeat(total, head_dim, axis=-1)).astype(bf16)
    log_total = peak + jnp.log(total)
    layer_out = (
        queries_in.astype(f32) + jnp.dot(attended, w_out, preferred_element_type=f32)
    ).astype(bf16)
    grad_att = lax.dot_general(
        grad_out, w_out, (((1,), (1,)), ((), ())), preferred_element_type=f32
    ).astype(bf16)
    grad_wo = jnp.einsum("qa,qb->ab", attended, grad_out, preferred_element_type=f32)
    deltas = jnp.sum(split_heads(grad_att).astype(f32) * split_heads(attended).astype(f32), axis=2)

    def backward_group(running, inputs):
        key_grad, value_grad = running
        query_rows, grad_rows, log_rows_g, delta_rows, block_rows = inputs
        allowed, scores = group_scores(query_rows, block_rows)
        attn_probs = jnp.where(allowed, jnp.exp(scores - log_rows_g[..., None]), 0.0)
        grad_heads = split_heads(grad_rows)
        value_grad = value_grad + jnp.einsum(
            "rhk,rhd->khd", attn_probs.astype(bf16), grad_heads, preferred_element_type=f32
        )
        grad_probs = jnp.einsum("rhd,khd->rhk", grad_heads, value_heads, preferred_element_type=f32)
        grad_scores = (attn_probs * (grad_probs - delta_rows[..., None]) * score_scale).astype(bf16)
        query_grad = jnp.einsum(
            "rhk,khd->rhd", grad_scores, key_heads, preferred_element_type=f32
        ).reshape(ROWS, width)
        key_grad = key_grad + jnp.einsum(
            "rhk,rhd->khd", grad_scores, split_heads(query_rows), preferred_element_type=f32
        )
        return ((key_grad, value_grad), query_grad)

    zero_grad = jnp.zeros((n_hits, HEADS, head_dim), f32)
    inputs_back = (
        query_groups,
        grad_att.reshape(groups, ROWS, width),
        log_total.reshape(groups, ROWS, HEADS),
        deltas.reshape(groups, ROWS, HEADS),
        column_groups,
    )
    (key_grad, value_grad), query_grad_parts = lax.scan(
        backward_group, (zero_grad, zero_grad), inputs_back
    )
    keys_grad = key_grad.reshape(n_hits, width).astype(bf16)
    vals_grad = value_grad.reshape(n_hits, width).astype(bf16)
    query_grad_local = query_grad_parts.reshape(n_queries, width)
    wk_part = jnp.einsum("ka,kb->ab", hits_in, keys_grad, preferred_element_type=f32)
    wv_part = jnp.einsum("ka,kb->ab", hits_in, vals_grad, preferred_element_type=f32)
    query_grad_sum, grad_wk, grad_wv = (
        lax.psum(query_grad_local.astype(jnp.bfloat16), "region").astype(jnp.float32),
        lax.psum(wk_part.astype(jnp.bfloat16), "region").astype(jnp.float32),
        lax.psum(wv_part.astype(jnp.bfloat16), "region").astype(jnp.float32),
    )
    grad_q = query_grad_sum.astype(bf16)
    grad_wq = jnp.einsum("qa,qb->ab", queries_in, grad_q, preferred_element_type=f32)
    grad_queries = (
        grad_out.astype(f32)
        + lax.dot_general(grad_q, w_query, (((1,), (1,)), ((), ())), preferred_element_type=f32)
    ).astype(bf16)
    grad_hits = (
        lax.dot_general(keys_grad, w_key, (((1,), (1,)), ((), ())), preferred_element_type=f32)
        + lax.dot_general(vals_grad, w_value, (((1,), (1,)), ((), ())), preferred_element_type=f32)
    ).astype(bf16)
    return (layer_out, grad_queries, grad_hits, grad_wq, grad_wk, grad_wv, grad_wo)


def solution(mesh):
    in_specs = (
        P("event", None),
        P(("event", "region"), None),
        P(),
        P(),
        P(),
        P(),
        P("event", None),
        P("event", None),
    )
    out_specs = (
        P("event", None),
        P("event", None),
        P(("event", "region"), None),
        P("event", None),
        P("event", None),
        P("event", None),
        P("event", None),
    )
    return jax.shard_map(
        on_device, mesh=mesh, in_specs=in_specs, out_specs=out_specs, check_vma=False
    )
```

profile of v0, /device:TPU:1, one launch (start us, length us, event | category | flops | bytes accessed | tf_op | source)
XLA Modules:
  0.0 878.9 jit_solution(16310437538966252421)
XLA Ops:
  15.3 48.3 %while.51 = (s32[]{:T(128)}, f32[2,512,512]{2,1,0:T(8,128)}, f32[2,512,8]{1,2,0:T(8,128)S(1)}, f32[2,512,8]{1,2,0:T(8,128)S(1)}, pred[2,4,1024]{2,1,0:T(4,128)(4...) while((s32[]{:T(128)}, f32[2,512,512]{2,1,0:T(8,128)}, ...), condition=%wide.region_4.5_spmd.clone, body=%wide.region_1.4_spmd.sunk.clone | while | flops 1128259584 | bytes 132788392 | solution.py:87
  19.6 6.6 fusion.117
  31.1 8.4 fusion.118
  43.8 6.6 fusion.117
  55.2 8.4 fusion.118
  67.1 43.9 %all-gather.6.cloned.1.call-done = f32[32,1024,8]{1,2,0:T(8,128)} async-done(((f32[1,1024,8]{1,2,0:T(8,128)}), f32[32,1024,8]{1,2,0:T(8,128)}) %all-gather.6.cloned.1.call-update) | async-done | bytes 1048592 | tf_op jit(solution)/shard_map/all_gather | solution.py:14
  111.8 44.2 %all-gather.8.cloned.1.call-done = f32[32,1024,8]{1,2,0:T(8,128)} async-done(((f32[1,1024,8]{1,2,0:T(8,128)}), f32[32,1024,8]{1,2,0:T(8,128)}) %all-gather.8.cloned.1.call-update) | async-done | bytes 1048592 | tf_op jit(solution)/shard_map/all_gather | solution.py:14
  156.8 201.9 %all-gather.4.cloned.1.call-done = f32[32,1024,512]{2,1,0:T(8,128)} async-done(((f32[1,1024,512]{2,1,0:T(8,128)}), f32[32,1024,512]{2,1,0:T(8,128)}) %all-gather.4.cloned.1.call-update) | async-done | bytes 67108880 | tf_op jit(solution)/shard_map/all_gather | solution.py:14
  364.7 289.0 %while.52 = (s32[]{:T(128)}, f32[1024,512]{0,1:T(8,128)}, f32[1024,8]{0,1:T(8,128)S(1)}, f32[1024,8]{0,1:T(8,128)S(1)}, f32[32,1024,8]{1,2,0:T(8,128)}, /*index=5*/f32[32,1024,512]{2,1,0:T(8,128)}, f32[32,1024,8]{1,2,0:T(8,128)}) while((s32[]{:T(128)}, f32[1024,512]{0,1:T(8,128)}, f32[1024,8]{0,1:T(8,128)S(1)}, ...), condition=%wide.region_6.7_spmd.clone, body=%wide.region_5.6_spmd.sunk.clone | while | flops 1622021 | bytes 15007871 | solution.py:20
  379.9 3.4 fusion.120
  389.3 3.4 fusion.120
  398.6 3.4 fusion.120
  407.9 3.4 fusion.120
  417.2 3.4 fusion.120
  426.5 3.4 fusion.120
  435.9 3.4 fusion.120
  445.2 3.4 fusion.120
  473.2 3.4 fusion.120
  482.5 3.4 fusion.120
  491.8 3.4 fusion.120
  501.1 3.4 fusion.120
  658.8 5.5 convert_multiply_fusion
  669.1 82.7 %while.53 = (s32[]{:T(128)}, f32[1024,8,64]{0,2,1:T(8,128)}, f32[1024,8,64]{0,2,1:T(8,128)}, bf16[2,512,512]{2,1,0:T(8,128)(2,1)}, bf16[2,512,512]{1,2,0:T(8,128...) while((s32[]{:T(128)}, f32[1024,8,64]{0,2,1:T(8,128)}, ...), condition=%wide.region_9.10_spmd.clone.clone, body=%wide.region_8.9_spmd.clone.sunk.clone | while | flops 2732589056 | bytes 144830800 | solution.py:130
  670.2 8.1 fusion.131
  679.5 12.4 %fusion.132 = bf16[512,8,1024]{2,0,1:T(8,128)(2,1)} fusion(f32[8,512,1024]{2,1,0:T(8,128)} %fusion.131, bf16[512,8,64]{0,2,1:T(8,128)(2,1)} %bitcast.259, bf16[1024,8,64]{0,2,1:T(8,128)(2,1)} %get-tuple-element.845, f32[512,8]{0,1:T(8,128)S(1)} %get-tuple-element.754, f32[512,8]{0,1:T(8,128)S(1)} %get-tuple-element.755, ...), kind=kOutput, calls=%fused_computation.31.clone.1.clone | convolution fusion | flops 566231040 | bytes 27295744 | tf_op jit(solution)/shard_map/while/body/eval_jaxpr/rhd,khd->rhk/dot_general | solution.py:112
  691.9 6.5 bitcast_add_fusion.6
  698.4 8.0 bitcast_add_fusion.7
  711.3 8.1 fusion.131
  720.6 12.4 %fusion.132 = bf16[512,8,1024]{2,0,1:T(8,128)(2,1)} fusion(f32[8,512,1024]{2,1,0:T(8,128)} %fusion.131, bf16[512,8,64]{0,2,1:T(8,128)(2,1)} %bitcast.259, bf16[1024,8,64]{0,2,1:T(8,128)(2,1)} %get-tuple-element.845, f32[512,8]{0,1:T(8,128)S(1)} %get-tuple-element.754, f32[512,8]{0,1:T(8,128)S(1)} %get-tuple-element.755, ...), kind=kOutput, calls=%fused_computation.31.clone.1.clone | convolution fusion | flops 566231040 | bytes 27295744 | tf_op jit(solution)/shard_map/while/body/eval_jaxpr/rhd,khd->rhk/dot_general | solution.py:112
  733.0 7.1 bitcast_add_fusion.6
  740.1 8.0 bitcast_add_fusion.7
  764.6 98.6 %all-reduce.3.cloned.1.call-done = (bf16[512,512]{0,1:T(8,128)(2,1)}, bf16[512,512]{0,1:T(8,128)(2,1)}, bf16[1024,512]{1,0:T(8,128)(2,1)}) async-done(((bf16[512,512]{0,1:T(8,128)(2,1)}, bf16[512,512]{0,1:T(8,128)(2,1)}, bf16[1024,512]{1,0:T(8,128)(2,1)}), (bf16[512,512]{0,1:T(8,128)(2,1)}, bf16[512,512]{0,1:T(8,128)(2,1)}, bf16[1024,512]{1,0:T(8,128)(2,1)})) %all-reduce.3.cloned.1.call-update) | async-done | bytes 2097168 | tf_op jit(solution)/shard_map/psum | solution.py:140
  (253 shorter events, 328.1 us)
Async XLA Ops:
  7.2 4.6 copy-start
  7.2 4.6 copy-start.9
  7.2 103.8 %all-gather.6.cloned.1.call-start = ((), (), s32[]{:S(2)}) async-start(), calls=%async_computation.1 | async-start | bytes 1081344 | tf_op jit(solution)/shard_map/all_gather | solution.py:14
  16.6 3.1 copy-start.19
  19.6 6.7 copy-start.1
  40.7 3.1 copy-start.19
  43.8 6.7 copy-start.1
  63.7 301.0 %copy-start.2 = (bf16[1024,8,64]{0,2,1:T(8,128)(2,1)}, bf16[1024,8,64]{0,2,1:T(8,128)(2,1)S(1)}, u32[]{:S(2)}) copy-start(bf16[1024,8,64]{0,2,1:T(8,128)(2,1)S(1)} %get-tuple-element.856) | copy-start | bytes 3145732
  64.3 91.7 %all-gather.8.cloned.1.call-start = ((), (), s32[]{:S(2)}) async-start(), calls=%async_computation.2 | async-start | bytes 1081344 | tf_op jit(solution)/shard_map/all_gather | solution.py:14
  65.1 293.6 %all-gather.4.cloned.1.call-start = ((), (), s32[]{:S(2)}) async-start(), calls=%async_computation | async-start | bytes 69206016 | tf_op jit(solution)/shard_map/all_gather | solution.py:14
  65.8 797.5 %all-reduce.3.cloned.1.call-start = ((), (), s32[]{:S(2)}) async-start(), calls=%async_computation.3 | async-start | bytes 4194304 | tf_op jit(solution)/shard_map/psum | solution.py:140
  664.3 4.8 copy-start.3
  670.2 8.1 copy-start.5
  691.9 6.5 copy-start.4
  691.9 6.5 copy-start.6
  691.9 14.5 %slice-start = ((s8[8388608]{0:T(1024)(128)(4,1)}), s8[4194304]{0:T(1024)(128)(4,1)S(1)}, s32[]{:S(2)}) async-start(s8[8388608]{0:T(1024)(128)(4,1)} %bitcast.249), calls=%async_computation.4 | async-start | bytes 8388608 | tf_op jit(solution)/shard_map/while
  698.4 8.0 slice-start.1
  706.4 2.7 copy-start.7
  711.3 8.1 copy-start.5
  733.0 7.1 copy-start.4
  733.0 7.1 copy-start.6
  733.0 15.1 %slice-start = ((s8[8388608]{0:T(1024)(128)(4,1)}), s8[4194304]{0:T(1024)(128)(4,1)S(1)}, s32[]{:S(2)}) async-start(s8[8388608]{0:T(1024)(128)(4,1)} %bitcast.249), calls=%async_computation.4 | async-start | bytes 8388608 | tf_op jit(solution)/shard_map/while
  740.1 8.0 slice-start.1
  748.1 2.7 copy-start.7
  751.8 3.4 copy-start.8
  756.9 3.4 copy-start.10
  757.0 4.2 copy-start.17
  757.0 4.2 copy-start.18
  757.0 4.2 copy-start.20
  761.2 102.1 %copy-start.16 = (bf16[1024,512]{1,0:T(8,128)(2,1)S(1)}, bf16[1024,512]{1,0:T(8,128)(2,1)}, u32[]{:S(2)}) copy-start(bf16[1024,512]{1,0:T(8,128)(2,1)} %param.21) | copy-start | bytes 3145732
  866.3 3.7 copy-start.13
  866.3 4.9 copy-start.12
  (3 other events, 3.8 us)
Sparse Core Ops, SparseCore 0:
  64.4 46.5 all-gather.5
  113.9 42.0 all-gather.7
  158.3 200.3 all-gather.3
  757.1 106.1 all-reduce.2
where the time goes:
time: 885 us; the launch traced here: 879 us
  waiting for transfers between devices  390 us (44%)
  local copies, waits for them, and re-layouts  197 us (22%)
  other arithmetic  155 us (18%)
  matrix products  122 us (14%)
  between operations  14 us (2%)
    all_gather x3, waiting for transfers between devices, merged(): everything = jax.tree.map(lambda part: lax.all_gather(part, axis), shard)  290 us
    dynamic_slice x62, local copies, waits for them, and re-layouts, lap(): return combine(so_far, jax.tree.map(lambda part: part[k], everything))  157 us
    add x31, other arithmetic, merge_partials(): numer_a * jnp.repeat(scale_a, head_dim, axis=-1)  107 us
    psum x1, waiting for transfers between devices, on_device(): lax.psum(wk_part.astype(jnp.bfloat16), 'region').astype(jnp.float32)  98.6 us
    add x31, other arithmetic, merge_partials(): return (numer, peak, total_a * scale_a + total_b * scale_b)  25.3 us
    dot_general x2, matrix products, backward_group(): jnp.einsum('rhd,khd->rhk', grad_heads, value_heads, preferred_element_typ...  24.8 us
    dot_general x4, matrix products, group_scores(): jnp.einsum('rhd,khd->rhk', split_heads(query_rows), key_heads, preferred_...  22.3 us
  transfers between devices with their start and end apart: 4, of which 4 were waited for; matrix products, arithmetic and copies ran while one was open for 1% of the time, Pallas kernels for 0%

commit v1 on v0

v1 whole, which is shorter than its diff:
```python
import jax
import jax.numpy as jnp
from jax import lax
from jax.experimental import pallas as pl
from jax.experimental.pallas import tpu as pltpu
from jax.sharding import PartitionSpec as P

f32 = jnp.float32
bf16 = jnp.bfloat16
HEADS = 8
PAIRS = 4
B = 128
QB = 8
HB = 8
D = 512
N = 1024
SCALE = 0.125
NEG = -1e30
VMEM_LIMIT = 60 * 1024 * 1024
MESH = pl.DeviceIdType.MESH
NN = (((1,), (0,)), ((), ()))
NT = (((1,), (1,)), ((), ()))
TN = (((0,), (0,)), ((), ()))


def dot(a, b, dims=NN):
    return lax.dot_general(a, b, dims, preferred_element_type=f32)


def transposed(block):
    return block.astype(f32).T.astype(block.dtype)


def pair_cols(p):
    return slice(p * B, (p + 1) * B)


def block_rows(i):
    return pl.ds(pl.multiple_of(i * B, B), B)


def read_mask(mask_ref, bits):
    first = lax.axis_index("region") * HB
    slot = mask_ref[...] - first
    inside = (slot >= 0) & (slot < HB)
    weight = jnp.where(inside, jnp.left_shift(1, jnp.clip(slot, 0, HB - 1)), 0).astype(f32)
    for qb in range(QB):
        bits[qb] = jnp.sum(weight[qb : qb + 1, :]).astype(jnp.int32)


def listed(bits, qb, hb):
    return (jnp.right_shift(bits[qb], hb) & 1) == 1


def lane_masks():
    lane = lax.broadcasted_iota(jnp.int32, (1, B), 1)
    even = jnp.where(lane < 64, 1.0, 0.0)
    return even.astype(bf16), (1.0 - even).astype(bf16)


def spread_heads(rows, p, out, masks):
    block = rows[:, pair_cols(p)]
    out[p, :B] = block * masks[0]
    out[p, B:] = block * masks[1]


def forward_kernel(queries, hits, w_query, w_key, w_value, mask_ref,
                   q_out, k_out, v_out, kt_out, even_out, odd_out,
                   vt, scores, heads_q, acc, peak, total, bits):
    read_mask(mask_ref, bits)
    masks = lane_masks()

    def project(i, _):
        rows = block_rows(i)
        k = dot(hits[rows, :], w_key[...]).astype(bf16)
        v = dot(hits[rows, :], w_value[...]).astype(bf16)
        k_out[rows, :] = k
        v_out[rows, :] = v
        kt_out[i] = transposed(k)
        vt[i] = transposed(v)
        q_out[rows, :] = (dot(queries[rows, :], w_query[...]) * SCALE).astype(bf16)
        return 0

    lax.fori_loop(0, 8, project, 0)

    def query_block(qb, _):
        rows = q_out[block_rows(qb), :]
        for p in range(PAIRS):
            spread_heads(rows, p, heads_q, masks)
        peak[...] = jnp.full(peak.shape, NEG, f32)
        total[...] = jnp.zeros(total.shape, f32)
        acc[...] = jnp.zeros(acc.shape, f32)

        def score_block(hb, _):
            @pl.when(listed(bits, qb, hb))
            def _():
                for p in range(PAIRS):
                    s = dot(k_out[block_rows(hb), pair_cols(p)], heads_q[p], NT)
                    scores[hb, p] = s
                    peak[p] = jnp.maximum(peak[p], jnp.max(s, axis=0, keepdims=True))

            return 0

        lax.fori_loop(0, HB, score_block, 0)

        def value_block(hb, _):
            @pl.when(listed(bits, qb, hb))
            def _():
                for p in range(PAIRS):
                    e = jnp.exp(scores[hb, p] - peak[p])
                    total[p] = total[p] + jnp.sum(e, axis=0, keepdims=True)
                    n = dot(vt[hb, pair_cols(p), :], e.astype(bf16))
                    acc[p, :64] = acc[p, :64] + n[:64, :B]
                    acc[p, 64:] = acc[p, 64:] + n[64:, B:]

            return 0

        lax.fori_loop(0, HB, value_block, 0)
        core, z = qb // 4, lax.rem(qb, 4)
        for p in range(PAIRS):
            for half, out in enumerate((even_out.at[core, p, z], odd_out.at[core, z, p])):
                lanes = slice(half * B, (half + 1) * B)
                out[:64] = acc[p, half * 64 : half * 64 + 64]
                out[64:72] = jnp.concatenate(
                    [peak[p, :, lanes], total[p, :, lanes], jnp.zeros((6, B), f32)], axis=0
                )
        return 0

    lax.fori_loop(0, QB, query_block, 0)


def place():
    r = lax.axis_index("region")
    return r // 8, lax.rem(r // 2, 4), lax.rem(r, 2)


def index_of(z, y, core):
    return (z * 4 + y) * 2 + core


def remote(src, dst, send, recv, peer):
    return pltpu.make_async_remote_copy(
        src_ref=src, dst_ref=dst, send_sem=send, recv_sem=recv,
        device_id={"region": peer}, device_id_type=MESH,
    )


def greet(peers):
    barrier = pltpu.get_barrier_semaphore()
    for peer in peers:
        pl.semaphore_signal(barrier, inc=1, device_id={"region": peer}, device_id_type=MESH)
    pl.semaphore_wait(barrier, len(peers))


def merge(parts):
    peak = parts[0][:, 64:65]
    for part in parts[1:]:
        peak = jnp.maximum(peak, part[:, 64:65])
    numer = total = None
    for part in parts:
        weight = jnp.exp(part[:, 64:65] - peak)
        n, t = part[:, :64] * weight, part[:, 65:66] * weight
        numer, total = (n, t) if numer is None else (numer + n, total + t)
    return numer, peak, total


def store_merged(ref, parts):
    numer, peak, total = merge(parts)
    ref[:, :64] = numer
    ref[:, 64:65] = peak
    ref[:, 65:66] = total


def softmax_kernel(even_in, odd_in, grad_out, w_out,
                   stats, gatt, attended,
                   pair_e, pair_o, half_e, half_o, first_e, first_o, quarter_e, quarter_o, second_e, second_o,
                   send, recv):
    z, y, core = place()
    sibling = index_of(z, y, 1 - core)
    ys = [lax.rem(y + i, 4) for i in (1, 2, 3)]
    zs = [lax.rem(z + i, 4) for i in (1, 2, 3)]
    y_peers = [index_of(z, v, core) for v in ys]
    z_peers = [index_of(v, y, core) for v in zs]
    cross = [index_of(z, v, 1 - core) for v in ys]
    greet([sibling] + y_peers + z_peers + cross)

    pair = [
        remote(src.at[1 - core], dst, send.at[i], recv.at[i], sibling)
        for i, (src, dst) in enumerate(((even_in, pair_e), (odd_in, pair_o)))
    ]
    for c in pair:
        c.start()

    def grad_att(i, _):
        rows = block_rows(i)
        gatt[rows, :] = dot(grad_out[rows, :], w_out[...], NT).astype(bf16)
        return 0

    lax.fori_loop(0, 8, grad_att, 0)

    stage1 = []
    for c, src, got, half, first, coords, peers, base in (
        (pair[0], even_in, pair_e, half_e, first_e, ys, y_peers, 2),
        (pair[1], odd_in, pair_o, half_o, first_o, zs, z_peers, 5),
    ):
        c.wait_recv()
        for j in range(4):
            store_merged(half.at[j], [src[core, j], got[j]])
        for i in range(3):
            d = remote(half.at[coords[i]], first.at[2 - i], send.at[base + i], recv.at[base + 2 - i], peers[i])
            d.start()
            stage1.append(d)
    stage2 = []
    for own, half, first, quarter, second, coords, peers, base, got in (
        (y, half_e, first_e, quarter_e, second_e, zs, z_peers, 8, 2),
        (z, half_o, first_o, quarter_o, second_o, ys, y_peers, 11, 5),
    ):
        for i in range(3):
            remote(first.at[i], first.at[i], send.at[got + i], recv.at[got + i], peers[i]).wait_recv()
        store_merged(quarter, [half[own], first[0], first[1], first[2]])
        for i in range(3):
            d = remote(quarter.at[coords[i]], second.at[2 - i], send.at[base + i], recv.at[base + 2 - i], peers[i])
            d.start()
            stage2.append(d)
    grads = gatt[block_rows(core * 4 + z), pl.ds(pl.multiple_of(y * B, B), B)].astype(f32).T
    tile = []
    logs, deltas = [], []
    for half, (own, quarter, second, got) in enumerate(
        ((z, quarter_e, second_e, 8), (y, quarter_o, second_o, 11))
    ):
        for i in range(3):
            remote(second.at[i], second.at[i], send.at[got + i], recv.at[got + i], sibling).wait_recv()
        numer, peak, total = merge([quarter[own][None], second[0:1], second[1:2], second[2:3]])
        att = (numer[0] / total[0]).astype(bf16).astype(f32)
        tile.append(att)
        logs.append(peak[0] + jnp.log(total[0]))
        deltas.append(jnp.sum(att * grads[half * 64 : half * 64 + 64], axis=0, keepdims=True))
    stats[z, y, core] = jnp.concatenate(logs + deltas + [jnp.zeros((4, B), f32)], axis=0)
    out = []
    mine = stats.at[z, y, core]
    for i, peer in enumerate([sibling] + y_peers + cross):
        slot = 0 if i == 0 else (3 - (i - 1) % 3) + (3 if i > 3 else 0)
        d = remote(mine, mine, send.at[14 + i], recv.at[14 + slot], peer)
        d.start()
        out.append(d)
    attended[...] = jnp.concatenate(tile, axis=0).T.astype(bf16)
    for i, (v, c) in enumerate([(y, 1 - core)] + [(v, core) for v in ys] + [(v, 1 - core) for v in ys]):
        there = stats.at[z, v, c]
        remote(there, there, send.at[14 + i], recv.at[14 + i], sibling).wait_recv()
    for i in range(3):
        d = remote(stats.at[z], stats.at[z], send.at[21 + i], recv.at[21 + 2 - i], z_peers[i])
        d.start()
        out.append(d)
    for i in range(3):
        there = stats.at[zs[i]]
        remote(there, there, send.at[21 + i], recv.at[21 + i], z_peers[i]).wait_recv()
    for d in pair + stage1 + stage2 + out:
        d.wait_send()


def backward_kernel(q, k, v, kt, gatt, stats, hits, w_key, w_value, mask_ref,
                    even_out, odd_out, grad_hits,
                    dk, dv, dkb, dvb, heads_q, heads_g, acc, bits):
    read_mask(mask_ref, bits)
    masks = lane_masks()
    dk[...] = jnp.zeros(dk.shape, f32)
    dv[...] = jnp.zeros(dv.shape, f32)

    def query_block(qb, _):
        core, z = qb // 4, lax.rem(qb, 4)
        rows, grads = q[block_rows(qb), :], gatt[block_rows(qb), :]
        for p in range(PAIRS):
            spread_heads(rows, p, heads_q, masks)
            spread_heads(grads, p, heads_g, masks)
        acc[...] = jnp.zeros(acc.shape, f32)

        def hit_block(hb, _):
            @pl.when(listed(bits, qb, hb))
            def _():
                here = block_rows(hb)
                for p in range(PAIRS):
                    cols = pair_cols(p)
                    stat = stats[z, p, core]
                    log_total = jnp.concatenate([stat[0:1], stat[1:2]], axis=1)
                    delta = jnp.concatenate([stat[2:3], stat[3:4]], axis=1)
                    s = dot(k[here, cols], heads_q[p], NT)
                    probs = jnp.exp(s - log_total)
                    dv[here, cols] += dot(probs.astype(bf16), heads_g[p])
                    dp = dot(v[here, cols], heads_g[p], NT)
                    ds = (probs * (dp - delta)).astype(bf16)
                    dk[here, cols] += dot(ds, heads_q[p])
                    n = dot(kt[hb, cols, :], ds)
                    acc[p, :64] = acc[p, :64] + n[:64, :B]
                    acc[p, 64:] = acc[p, 64:] + n[64:, B:]

            return 0

        lax.fori_loop(0, HB, hit_block, 0)
        for p in range(PAIRS):
            even_out[core, p, z, :64] = (acc[p, :64] * SCALE).astype(bf16)
            odd_out[core, z, p, :64] = (acc[p, 64:] * SCALE).astype(bf16)
        return 0

    lax.fori_loop(0, QB, query_block, 0)

    def finish(i, _):
        rows = block_rows(i)
        a, b = dk[rows, :].astype(bf16), dv[rows, :].astype(bf16)
        dkb[rows, :] = a
        dvb[rows, :] = b
        grad_hits[rows, :] = (dot(a, w_key[...], NT) + dot(b, w_value[...], NT)).astype(bf16)
        return 0

    lax.fori_loop(0, 8, finish, 0)
    for which, grad in enumerate((dkb, dvb)):
        for z in range(4):
            part = dot(hits[:, z * B : (z + 1) * B], grad[...], TN).astype(bf16)
            for p in range(PAIRS):
                even_out[which, p, z, 64:] = part[:64, pair_cols(p)]
                odd_out[which, z, p, 64:] = part[64:, pair_cols(p)]


def total_kernel(even_in, odd_in, attended,
                 gath_a, gath_b,
                 pair_e, pair_o, half_e, half_o, first_e, first_o, quarter_e, quarter_o, second_e, second_o,
                 send, recv):
    z, y, core = place()
    sibling = index_of(z, y, 1 - core)
    ys = [lax.rem(y + i, 4) for i in (1, 2, 3)]
    zs = [lax.rem(z + i, 4) for i in (1, 2, 3)]
    y_peers = [index_of(z, v, core) for v in ys]
    z_peers = [index_of(v, y, core) for v in zs]
    greet([sibling] + y_peers + z_peers)
    sent = []

    def go(src, dst, s, r, peer):
        d = remote(src, dst, send.at[s], recv.at[r], peer)
        d.start()
        sent.append(d)

    def got(ref, r):
        remote(ref, ref, send.at[r], recv.at[r], sibling).wait_recv()

    for i, (src, dst) in enumerate(((even_in, pair_e), (odd_in, pair_o))):
        go(src.at[1 - core], dst, i, i, sibling)
    for src, pair, half, first, coords, peers, base, i0 in (
        (even_in, pair_e, half_e, first_e, ys, y_peers, 2, 0),
        (odd_in, pair_o, half_o, first_o, zs, z_peers, 5, 1),
    ):
        got(pair, i0)
        for j in range(4):
            half[j] = (src[core, j].astype(f32) + pair[j].astype(f32)).astype(bf16)
        for i in range(3):
            go(half.at[coords[i]], first.at[2 - i], base + i, base + 2 - i, peers[i])
    for own, half, first, quarter, second, coords, peers, base, before in (
        (y, half_e, first_e, quarter_e, second_e, zs, z_peers, 8, 2),
        (z, half_o, first_o, quarter_o, second_o, ys, y_peers, 11, 5),
    ):
        for i in range(3):
            got(first.at[i], before + i)
        total = half[own].astype(f32)
        for i in range(3):
            total = total + first[i].astype(f32)
        quarter[...] = total.astype(bf16)
        for i in range(3):
            go(quarter.at[coords[i]], second.at[2 - i], base + i, base + 2 - i, peers[i])
    sums = []
    for own, quarter, second, before in ((z, quarter_e, second_e, 8), (y, quarter_o, second_o, 11)):
        for i in range(3):
            got(second.at[i], before + i)
        total = quarter[own].astype(f32)
        for i in range(3):
            total = total + second[i].astype(f32)
        sums.append(total)
    grad_q = jnp.concatenate([sums[0][:64], sums[1][:64]], axis=0).T.astype(bf16)
    att = attended[...]
    blocks = []
    for half, gath in enumerate((gath_a.at[core, z, y], gath_b.at[core, y, z])):
        rows = slice(half * 64, half * 64 + 64)
        gath[:64] = grad_q[rows]
        gath[64:128] = sums[half][64:].astype(bf16)
        gath[128:] = att[rows]
        blocks.append(gath)
    for i in range(3):
        go(blocks[0], blocks[0], 14 + i, 14 + 2 - i, y_peers[i])
        go(blocks[1], blocks[1], 17 + i, 17 + 2 - i, z_peers[i])
    for i in range(3):
        got(gath_a.at[core, z, ys[i]], 14 + i)
        got(gath_b.at[core, y, zs[i]], 17 + i)
    for i in range(3):
        go(gath_a.at[core, z], gath_a.at[core, z], 20 + i, 20 + 2 - i, z_peers[i])
        go(gath_b.at[core, y], gath_b.at[core, y], 23 + i, 23 + 2 - i, y_peers[i])
    go(gath_a.at[core, z], gath_a.at[core, z], 26, 26, sibling)
    go(gath_b.at[core, y], gath_b.at[core, y], 27, 27, sibling)
    for i in range(3):
        got(gath_a.at[core, zs[i]], 20 + i)
        go(gath_a.at[core, zs[i]], gath_a.at[core, zs[i]], 28 + i, 28 + i, sibling)
        got(gath_b.at[core, ys[i]], 23 + i)
        go(gath_b.at[core, ys[i]], gath_b.at[core, ys[i]], 31 + i, 31 + i, sibling)
    got(gath_a.at[1 - core, z], 26)
    got(gath_b.at[1 - core, y], 27)
    for i in range(3):
        got(gath_a.at[1 - core, zs[i]], 28 + i)
        got(gath_b.at[1 - core, ys[i]], 31 + i)
    for d in sent:
        d.wait_send()


def final_kernel(queries, grad_out, w_query, w_out, gath_a, gath_b,
                 layer_out, grad_queries, grad_wq, grad_wk, grad_wv, grad_wo,
                 grad_q, attended):
    for qb in range(QB):
        core, z = qb // 4, qb % 4
        for p in range(PAIRS):
            for half in range(2):
                block = gath_a.at[core, z, p] if half == 0 else gath_b.at[core, p, z]
                rows = slice(qb * B + half * 64, qb * B + half * 64 + 64)
                grad_q[rows, pair_cols(p)] = block[:64]
                attended[rows, pair_cols(p)] = block[128:]
                out = grad_wk if core == 0 else grad_wv
                local = slice(z * B + half * 64, z * B + half * 64 + 64)
                out[local, pair_cols(p)] = block[64:128].astype(f32)

    def rows_block(i, _):
        rows = block_rows(i)
        layer_out[rows, :] = (queries[rows, :].astype(f32) + dot(attended[rows, :], w_out[...])).astype(bf16)
        grad_queries[rows, :] = (grad_out[rows, :].astype(f32) + dot(grad_q[rows, :], w_query[...], NT)).astype(bf16)
        return 0

    lax.fori_loop(0, 8, rows_block, 0)
    for j in range(4):
        cols = pair_cols(j)
        grad_wq[cols, :] = dot(queries[:, cols], grad_q[...], TN)
        grad_wo[cols, :] = dot(attended[:, cols], grad_out[...], TN)


def shaped(*shape, dtype=f32):
    return jax.ShapeDtypeStruct(shape, dtype)


def call(kernel, args, outs, scratch, collective=None):
    in_vmem = pl.BlockSpec(memory_space=pltpu.VMEM)
    params = {"vmem_limit_bytes": VMEM_LIMIT}
    if collective is not None:
        params |= {"collective_id": collective, "has_side_effects": True}
    return pl.pallas_call(
        kernel,
        out_shape=outs,
        in_specs=[in_vmem] * len(args),
        out_specs=tuple([in_vmem] * len(outs)),
        scratch_shapes=scratch,
        compiler_params=pltpu.CompilerParams(**params),
        name=kernel.__name__,
    )(*args)


def stages(rows, dtype):
    shapes = []
    for lead in ((4, 4), (4, 4), (3, 4), (4,), (3,)):
        shapes += [pltpu.VMEM(lead + (rows, B), dtype)] * 2
    return shapes


def on_device(queries_in, hits_in, w_query, w_key, w_value, w_out, mask_list, grad_out):
    q, k, v, kt, even, odd = call(
        forward_kernel,
        (queries_in, hits_in, w_query, w_key, w_value, mask_list),
        (
            shaped(N, D, dtype=bf16), shaped(N, D, dtype=bf16), shaped(N, D, dtype=bf16),
            shaped(HB, D, B, dtype=bf16), shaped(2, 4, 4, 72, B), shaped(2, 4, 4, 72, B),
        ),
        [
            pltpu.VMEM((HB, D, B), bf16),
            pltpu.VMEM((HB, PAIRS, B, 2 * B), f32),
            pltpu.VMEM((PAIRS, 2 * B, B), bf16),
            pltpu.VMEM((PAIRS, B, B), f32),
            pltpu.VMEM((PAIRS, 1, 2 * B), f32),
            pltpu.VMEM((PAIRS, 1, 2 * B), f32),
            pltpu.SMEM((QB,), jnp.int32),
        ],
    )
    stats, gatt, attended = call(
        softmax_kernel,
        (even, odd, grad_out, w_out),
        (shaped(4, 4, 2, 8, B), shaped(N, D, dtype=bf16), shaped(B, B, dtype=bf16)),
        stages(72, f32) + [pltpu.SemaphoreType.DMA((24,)), pltpu.SemaphoreType.DMA((24,))],
        collective=0,
    )
    even, odd, grad_hits = call(
        backward_kernel,
        (q, k, v, kt, gatt, stats, hits_in, w_key, w_value, mask_list),
        (shaped(2, 4, 4, B, B, dtype=bf16), shaped(2, 4, 4, B, B, dtype=bf16), shaped(N, D, dtype=bf16)),
        [
            pltpu.VMEM((N, D), f32), pltpu.VMEM((N, D), f32),
            pltpu.VMEM((N, D), bf16), pltpu.VMEM((N, D), bf16),
            pltpu.VMEM((PAIRS, 2 * B, B), bf16), pltpu.VMEM((PAIRS, 2 * B, B), bf16),
            pltpu.VMEM((PAIRS, B, B), f32),
            pltpu.SMEM((QB,), jnp.int32),
        ],
    )
    gath_a, gath_b = call(
        total_kernel,
        (even, odd, attended),
        (shaped(2, 4, 4, 192, B, dtype=bf16), shaped(2, 4, 4, 192, B, dtype=bf16)),
        stages(B, bf16) + [pltpu.SemaphoreType.DMA((34,)), pltpu.SemaphoreType.DMA((34,))],
        collective=1,
    )
    layer_out, grad_queries, grad_wq, grad_wk, grad_wv, grad_wo = call(
        final_kernel,
        (queries_in, grad_out, w_query, w_out, gath_a, gath_b),
        (
            shaped(N, D, dtype=bf16), shaped(N, D, dtype=bf16),
            shaped(D, D), shaped(D, D), shaped(D, D), shaped(D, D),
        ),
        [pltpu.VMEM((N, D), bf16), pltpu.VMEM((N, D), bf16)],
    )
    return (layer_out, grad_queries, grad_hits, grad_wq, grad_wk, grad_wv, grad_wo)


def solution(mesh):
    per_event = P("event", None)
    per_region = P(("event", "region"), None)
    return jax.shard_map(
        on_device,
        mesh=mesh,
        in_specs=(per_event, per_region, P(), P(), P(), P(), per_event, per_event),
        out_specs=(per_event, per_event, per_region, per_event, per_event, per_event, per_event),
        check_vma=False,
    )
```

time: 885 us -> 140 us (0.16)
  the two profiles are of different devices: /device:TPU:1 before, /device:TPU:3 now
where the time goes in v1:
time: 140 us
  Pallas kernels  139 us (99%)
    pallas_call x5, Pallas kernels, call(): pl.pallas_call(kernel, out_shape=outs, in_specs=[in_vmem] * len(args), ou...  139 us

profile of v1, /device:TPU:3, one launch (start us, length us, event | category | flops | bytes accessed | tf_op | source)
XLA Modules:
  0.0 139.6 jit_solution(7803372382062070409)
XLA Ops:
  0.6 20.2 %forward_kernel.1 = (bf16[1024,512]{1,0:T(8,128)(2,1)}, bf16[1024,512]{1,0:T(8,128)(2,1)}, bf16[1024,512]{1,0:T(8,128)(2,1)}, bf16[8,512,128]{2,1,0:T(8,128)(2,1...) custom-call(bf16[1024,512]{1,0:T(8,128)(2,1)} %queries.3, bf16[1024,512]{1,0:T(8,128)(2,1)} %hits.3, ...), custom_call_target="tpu_custom_call" | custom-call | tf_op jit(solution)/shard_map/forward_kernel/pallas_call | solution.py:446
  20.8 34.8 %softmax_kernel.1 = (f32[4,4,2,8,128]{4,3,2,1,0:T(8,128)}, bf16[1024,512]{1,0:T(8,128)(2,1)}, bf16[128,128]{1,0:T(8,128)(2,1)}) custom-call(f32[2,4,4,72,128]{4,3,2,1,0:T(8,128)} %get-tuple-element.31.even_in, f32[2,4,4,72,128]{4,3,2,1,0:T(8,128)} %get-tuple-element.32.odd_in, bf16[1024,512]{1,0:T(8,128)(2,1)} %grad_out.3, bf16[512,512]{1,0:T(8,128)(2,1)} %w_out.3), custom_call_target="tpu_custom_call" | custom-call | tf_op jit(solution)/shard_map/softmax_kernel/pallas_call | solution.py:446
  55.6 33.1 %backward_kernel.1 = (bf16[2,4,4,128,128]{4,3,2,1,0:T(8,128)(2,1)}, bf16[2,4,4,128,128]{4,3,2,1,0:T(8,128)(2,1)}, bf16[1024,512]{1,0:T(8,128)(2,1)}) custom-call(bf16[1024,512]{1,0:T(8,128)(2,1)} %get-tuple-element.27.q, bf16[1024,512]{1,0:T(8,128)(2,1)} %get-tuple-element.28.k, bf16[1024,512]{1,0:T(8,128)(2,1)} %get-tuple-element.29.v, ...), custom_call_target="tpu_custom_call" | custom-call | tf_op jit(solution)/shard_map/backward_kernel/pallas_call | solution.py:446
  88.7 41.9 %total_kernel.1 = (bf16[2,4,4,192,128]{4,3,2,1,0:T(8,128)(2,1)}, bf16[2,4,4,192,128]{4,3,2,1,0:T(8,128)(2,1)}) custom-call(bf16[2,4,4,128,128]{4,3,2,1,0:T(8,128)(2,1)} %get-tuple-element.35.even_in, bf16[2,4,4,128,128]{4,3,2,1,0:T(8,128)(2,1)} %get-tuple-element.36.odd_in, bf16[128,128]{1,0:T(8,128)(2,1)} %get-tuple-element.37.attended), custom_call_target="tpu_custom_call" | custom-call | tf_op jit(solution)/shard_map/total_kernel/pallas_call | solution.py:446
  130.6 9.0 %final_kernel.1 = (bf16[1024,512]{1,0:T(8,128)(2,1)}, bf16[1024,512]{1,0:T(8,128)(2,1)}, f32[512,512]{1,0:T(8,128)}, f32[512,512]{1,0:T(8,128)}, f32[512,512]{1,0:T(8,128)}, /*index=5*/f32[512,512]{1,0:T(8,128)}) custom-call(bf16[1024,512]{1,0:T(8,128)(2,1)} %queries.3, bf16[1024,512]{1,0:T(8,128)(2,1)} %grad_out.3, bf16[512,512]{1,0:T(8,128)(2,1)} %w_query.3, ...), custom_call_target="tpu_custom_call" | custom-call | tf_op jit(solution)/shard_map/final_kernel/pallas_call | solution.py:446

commit v2 on v1

v2 whole, which is shorter than its diff:
```python
import jax
import jax.numpy as jnp
from jax import lax
from jax.experimental import pallas as pl
from jax.experimental.pallas import tpu as pltpu
from jax.sharding import PartitionSpec as P

f32 = jnp.float32
bf16 = jnp.bfloat16
HEADS = 8
PAIRS = 4
B = 128
QB = 8
HB = 8
D = 512
N = 1024
SCALE = 0.125
NEG = -1e30
VMEM_LIMIT = 60 * 1024 * 1024
MESH = pl.DeviceIdType.MESH
NN = (((1,), (0,)), ((), ()))
NT = (((1,), (1,)), ((), ()))
TN = (((0,), (0,)), ((), ()))


def dot(a, b, dims=NN):
    return lax.dot_general(a, b, dims, preferred_element_type=f32)


def transposed(block):
    return block.astype(f32).T.astype(block.dtype)


def pair_cols(p):
    return slice(p * B, (p + 1) * B)


def block_rows(i):
    return pl.ds(pl.multiple_of(i * B, B), B)


def list_blocks(mask_ref, lists, counts):
    first = lax.axis_index("region") * HB
    slot = mask_ref[...] - first
    inside = (slot >= 0) & (slot < HB)
    weight = jnp.where(inside, jnp.left_shift(1, jnp.clip(slot, 0, HB - 1)), 0).astype(f32)
    for qb in range(QB):
        bits = jnp.sum(weight[qb : qb + 1, :]).astype(jnp.int32)
        count = jnp.int32(0)
        for hb in range(HB):
            lists[qb, count] = hb
            count = count + (jnp.right_shift(bits, hb) & 1)
        counts[qb] = count


def over_listed(lists, counts, qb, body):
    count = counts[qb]

    def two(i, _):
        body([lists[qb, 2 * i], lists[qb, 2 * i + 1]])
        return 0

    lax.fori_loop(0, count // 2, two, 0)

    @pl.when(lax.rem(count, 2) == 1)
    def _():
        body([lists[qb, count - 1]])


def gathered_rows(ref, blocks, cols):
    return jnp.concatenate([ref[block_rows(b), cols] for b in blocks], axis=0)


def gathered_cols(ref, blocks, rows):
    return jnp.concatenate([ref[b, rows, :] for b in blocks], axis=1)


def lane_masks():
    lane = lax.broadcasted_iota(jnp.int32, (1, B), 1)
    even = jnp.where(lane < 64, 1.0, 0.0)
    return even.astype(bf16), (1.0 - even).astype(bf16)


def spread_heads(rows, p, out, masks):
    block = rows[:, pair_cols(p)]
    out[p, :B] = block * masks[0]
    out[p, B:] = block * masks[1]


def loads(pairs, sems):
    copies = [pltpu.make_async_copy(src, dst, sems.at[i]) for i, (src, dst) in enumerate(pairs)]
    for c in copies:
        c.start()
    return copies


def forward_kernel(queries_h, hits_h, w_query_h, w_key_h, w_value_h, grad_out_h, w_out_h, mask_ref,
                   q_h, k_h, v_h, natt_e, natt_o, stats,
                   queries, hits, w_query, w_key, w_value, grad_out, w_out, q, k, v,
                   vt, gatt_t, heads_q, acc, peak, total, lists, counts, sems_in, sems_out):
    ins = loads(
        ((hits_h, hits), (w_value_h, w_value), (w_key_h, w_key), (queries_h, queries),
         (w_query_h, w_query), (grad_out_h, grad_out), (w_out_h, w_out)), sems_in)
    list_blocks(mask_ref, lists, counts)
    masks = lane_masks()
    outs = []

    def project(src, weight, out, scale=None):
        def part(i, _):
            rows = pl.ds(pl.multiple_of(i * 256, 256), 256)
            x = dot(src[rows, :], weight[...])
            out[rows, :] = (x if scale is None else x * scale).astype(bf16)
            return 0

        lax.fori_loop(0, 4, part, 0)

    def save(i, src, dst):
        c = pltpu.make_async_copy(src, dst, sems_out.at[i])
        c.start()
        outs.append(c)

    ins[0].wait()
    ins[1].wait()
    project(hits, w_value, v)
    save(0, v, v_h)

    def turn(i, _):
        vt[i] = transposed(v[block_rows(i), :])
        return 0

    lax.fori_loop(0, HB, turn, 0)
    ins[2].wait()
    project(hits, w_key, k)
    save(1, k, k_h)
    ins[3].wait()
    ins[4].wait()
    project(queries, w_query, q, SCALE)
    save(2, q, q_h)
    ins[5].wait()
    ins[6].wait()

    def grads(i, _):
        x = dot(w_out[...], grad_out[pl.ds(pl.multiple_of(i * 256, 256), 256), :], NT).astype(bf16)
        gatt_t[2 * i] = x[:, :B]
        gatt_t[2 * i + 1] = x[:, B:]
        return 0

    lax.fori_loop(0, 4, grads, 0)

    def query_block(qb, _):
        rows = q[block_rows(qb), :]
        for p in range(PAIRS):
            spread_heads(rows, p, heads_q, masks)
        peak[...] = jnp.full(peak.shape, NEG, f32)
        total[...] = jnp.zeros(total.shape, f32)
        acc[...] = jnp.zeros(acc.shape, f32)

        def body(blocks):
            ps = range(PAIRS)
            scores = [dot(gathered_rows(k, blocks, pair_cols(p)), heads_q[p], NT) for p in ps]
            old = [peak[p] for p in ps]
            new = [jnp.maximum(o, jnp.max(s, axis=0, keepdims=True)) for o, s in zip(old, scores)]
            shrink = [jnp.exp(o - n) for o, n in zip(old, new)]
            expo = [jnp.exp(s - n) for s, n in zip(scores, new)]
            numer = [dot(gathered_cols(vt, blocks, pair_cols(p)), expo[p].astype(bf16)) for p in ps]
            for p in ps:
                peak[p] = new[p]
                total[p] = total[p] * shrink[p] + jnp.sum(expo[p], axis=0, keepdims=True)
                acc[p, :64] = acc[p, :64] * shrink[p][:, :B] + numer[p][:64, :B]
                acc[p, 64:] = acc[p, 64:] * shrink[p][:, B:] + numer[p][64:, B:]

        over_listed(lists, counts, qb, body)
        core, z = qb // 4, lax.rem(qb, 4)
        for p in range(PAIRS):
            some = total[p] > 0.0
            safe = jnp.where(some, total[p], 1.0)
            log_total = jnp.where(some, peak[p] + jnp.log(safe), NEG)
            inverse = 1.0 / safe
            for half, out in enumerate((natt_e.at[core, p, z], natt_o.at[core, z, p])):
                lanes = slice(half * B, (half + 1) * B)
                rows = slice(half * 64, half * 64 + 64)
                part = acc[p, rows] * inverse[:, lanes]
                out[...] = part.astype(bf16)
                grads = gatt_t[qb, p * B + half * 64 : p * B + half * 64 + 64, :].astype(f32)
                h = 2 * p + half
                stats[qb, h : h + 1, :] = log_total[:, lanes]
                stats[qb, 8 + h : 9 + h, :] = jnp.sum(part * grads, axis=0, keepdims=True)
        return 0

    lax.fori_loop(0, QB, query_block, 0)
    for c in outs:
        c.wait()


def place():
    r = lax.axis_index("region")
    return r // 8, lax.rem(r // 2, 4), lax.rem(r, 2)


def index_of(z, y, core):
    return (z * 4 + y) * 2 + core


def remote(src, dst, send, recv, peer):
    return pltpu.make_async_remote_copy(
        src_ref=src, dst_ref=dst, send_sem=send, recv_sem=recv,
        device_id={"region": peer}, device_id_type=MESH,
    )


def greet(peers):
    barrier = pltpu.get_barrier_semaphore()
    for peer in peers:
        pl.semaphore_signal(barrier, inc=1, device_id={"region": peer}, device_id_type=MESH)
    pl.semaphore_wait(barrier, len(peers))


class Links:
    def __init__(self, send, recv):
        self.send, self.recv, self.sent = send, recv, []

    def go(self, src, dst, s, r, peer):
        d = remote(src, dst, self.send.at[s], self.recv.at[r], peer)
        d.start()
        self.sent.append(d)

    def got(self, ref, r, peer):
        remote(ref, ref, self.send.at[r], self.recv.at[r], peer).wait_recv()

    def finish(self):
        for d in self.sent:
            d.wait_send()


def merge(parts):
    peak = parts[0][:, :8]
    for part in parts[1:]:
        peak = jnp.maximum(peak, part[:, :8])
    total = None
    for part in parts:
        w = jnp.exp(part[:, :8] - peak)
        total = w if total is None else total + w
    log_total = peak + jnp.log(total)
    delta = None
    for part in parts:
        d = part[:, 8:] * jnp.exp(part[:, :8] - log_total)
        delta = d if delta is None else delta + d
    return jnp.concatenate([log_total, delta], axis=1)


def softmax_kernel(stats_in, k_h, hits_h, grad_out_h, w_out_h,
                   stats, kt_h, hits_t_h, gatt_h,
                   pair, half_a, half_b, got_a1, got_b1, mid_a, mid_b, got_a2, got_b2,
                   k, hits, grad_out, w_out, kt, hits_t, gatt, send, recv, sems_in, sems_out):
    z, y, core = place()
    sibling = index_of(z, y, 1 - core)
    ys = [lax.rem(y + i, 4) for i in (1, 2, 3)]
    zs = [lax.rem(z + i, 4) for i in (1, 2, 3)]
    y_peers = [index_of(z, v, core) for v in ys]
    z_peers = [index_of(v, y, core) for v in zs]
    ins = loads(((grad_out_h, grad_out), (w_out_h, w_out), (k_h, k), (hits_h, hits)), sems_in)
    greet([sibling] + y_peers + z_peers)
    net = Links(send, recv)
    theirs, mine = pl.ds(4 * (1 - core), 4), 4 * core
    net.go(stats_in.at[theirs], pair, 0, 0, sibling)
    outs = []

    def save(i, src, dst):
        c = pltpu.make_async_copy(src, dst, sems_out.at[i])
        c.start()
        outs.append(c)

    def grad_att(i):
        rows = slice(i * 256, i * 256 + 256)
        gatt[rows, :] = dot(grad_out[rows, :], w_out[...], NT).astype(bf16)

    def turn(src, dst, first, count):
        def one(i, _):
            dst[i] = transposed(src[block_rows(i), :])
            return 0

        lax.fori_loop(first, first + count, one, 0)

    net.got(pair, 0, sibling)
    half_a[...] = merge([stats_in[pl.ds(mine, 2)], pair[:2]])
    half_b[...] = merge([stats_in[pl.ds(mine + 2, 2)], pair[2:]])
    for i in range(3):
        net.go(half_a, got_a1.at[2 - i], 1 + i, 1 + 2 - i, y_peers[i])
        net.go(half_b, got_b1.at[2 - i], 4 + i, 4 + 2 - i, z_peers[i])
    ins[0].wait()
    ins[1].wait()
    grad_att(0)
    grad_att(1)
    for i in range(3):
        net.got(got_a1.at[i], 1 + i, y_peers[i])
        net.got(got_b1.at[i], 4 + i, z_peers[i])
    mid_a[...] = merge([half_a[...], got_a1[0], got_a1[1], got_a1[2]])
    mid_b[...] = merge([half_b[...], got_b1[0], got_b1[1], got_b1[2]])
    for i in range(3):
        net.go(mid_a, got_a2.at[2 - i], 7 + i, 7 + 2 - i, z_peers[i])
        net.go(mid_b, got_b2.at[2 - i], 10 + i, 10 + 2 - i, y_peers[i])
    grad_att(2)
    grad_att(3)
    save(0, gatt, gatt_h)
    for c in ins[2:]:
        c.wait()
    turn(k, kt, 0, 4)
    for i in range(3):
        net.got(got_a2.at[i], 7 + i, z_peers[i])
        net.got(got_b2.at[i], 10 + i, y_peers[i])
    stats[pl.ds(mine, 2)] = merge([mid_a[...], got_a2[0], got_a2[1], got_a2[2]])
    stats[pl.ds(mine + 2, 2)] = merge([mid_b[...], got_b2[0], got_b2[1], got_b2[2]])
    here = stats.at[pl.ds(mine, 4)]
    net.go(here, here, 13, 13, sibling)
    turn(k, kt, 4, 4)
    save(1, kt, kt_h)
    turn(hits, hits_t, 0, 8)
    save(2, hits_t, hits_t_h)
    net.got(stats.at[theirs], 13, sibling)
    net.finish()
    for c in outs:
        c.wait()


def backward_kernel(q, k, v, kt, gatt, stats, stats_own, natt_e, natt_o, hits_t_h, w_key_h, w_value_h, mask_ref,
                    even_out, odd_out, grad_hits,
                    hits_t, w_key, w_value, dk, dv, dkb, dvb, heads_q, heads_g, acc, lists, counts, sems_in):
    ins = loads(((w_key_h, w_key), (w_value_h, w_value), (hits_t_h, hits_t)), sems_in)
    list_blocks(mask_ref, lists, counts)
    masks = lane_masks()
    dk[...] = jnp.zeros(dk.shape, f32)
    dv[...] = jnp.zeros(dv.shape, f32)

    def query_block(qb, _):
        core, z = qb // 4, lax.rem(qb, 4)
        rows, grads = q[block_rows(qb), :], gatt[block_rows(qb), :]
        for p in range(PAIRS):
            spread_heads(rows, p, heads_q, masks)
            spread_heads(grads, p, heads_g, masks)
        acc[...] = jnp.zeros(acc.shape, f32)

        def stat_row(p, base):
            h = base + 2 * p
            return jnp.concatenate([stats[qb, h : h + 1, :], stats[qb, h + 1 : h + 2, :]], axis=1)

        def body(blocks):
            ps = range(PAIRS)
            keys = [gathered_rows(k, blocks, pair_cols(p)) for p in ps]
            vals = [gathered_rows(v, blocks, pair_cols(p)) for p in ps]
            scores = [dot(keys[p], heads_q[p], NT) for p in ps]
            dps = [dot(vals[p], heads_g[p], NT) for p in ps]
            probs = [jnp.exp(scores[p] - stat_row(p, 0)) for p in ps]
            ds = [(probs[p] * (dps[p] - stat_row(p, 8))).astype(bf16) for p in ps]
            dvs = [dot(probs[p].astype(bf16), heads_g[p]) for p in ps]
            dks = [dot(ds[p], heads_q[p]) for p in ps]
            dqs = [dot(gathered_cols(kt, blocks, pair_cols(p)), ds[p]) for p in ps]
            for p in ps:
                for j, b in enumerate(blocks):
                    part = slice(j * B, (j + 1) * B)
                    dv[block_rows(b), pair_cols(p)] += dvs[p][part]
                    dk[block_rows(b), pair_cols(p)] += dks[p][part]
                acc[p, :64] = acc[p, :64] + dqs[p][:64, :B]
                acc[p, 64:] = acc[p, 64:] + dqs[p][64:, B:]

        over_listed(lists, counts, qb, body)
        for p in range(PAIRS):
            for half, (out, natt) in enumerate(
                ((even_out.at[:, core, p, z], natt_e.at[core, p, z]), (odd_out.at[:, core, z, p], natt_o.at[core, z, p]))
            ):
                h = 2 * p + half
                weight = jnp.exp(stats_own[qb, h : h + 1, :] - stats[qb, h : h + 1, :])
                out[0, :64] = (natt[...].astype(f32) * weight).astype(bf16)
                out[1, :64] = (acc[p, half * 64 : half * 64 + 64] * SCALE).astype(bf16)
        return 0

    lax.fori_loop(0, QB, query_block, 0)
    ins[0].wait()
    ins[1].wait()

    def finish(i, _):
        rows = pl.ds(pl.multiple_of(i * 256, 256), 256)
        a, b = dk[rows, :].astype(bf16), dv[rows, :].astype(bf16)
        dkb[rows, :] = a
        dvb[rows, :] = b
        grad_hits[rows, :] = (dot(a, w_key[...], NT) + dot(b, w_value[...], NT)).astype(bf16)
        return 0

    lax.fori_loop(0, 4, finish, 0)
    ins[2].wait()
    for which, grad in enumerate((dkb, dvb)):
        for z in range(4):
            rows = jnp.concatenate([hits_t[i, z * B : (z + 1) * B, :] for i in range(HB)], axis=1)
            part = dot(rows, grad[...]).astype(bf16)
            for p in range(PAIRS):
                for chunk in range(2):
                    lo = 32 * chunk
                    even_out[chunk, which, p, z, 64:] = part[lo : lo + 32, pair_cols(p)]
                    odd_out[chunk, which, z, p, 64:] = part[64 + lo : 96 + lo, pair_cols(p)]


HALVES = (slice(0, 48), slice(48, 96))
FLOWS = 42


def total_kernel(even_in, odd_in, gath_a, gath_b,
                 pair_e, pair_o, half_e, half_o, relay_e, relay_o, near_e, near_o,
                 quarter_e, quarter_o, second_e, second_o, send, recv):
    z, y, core = place()
    sibling = index_of(z, y, 1 - core)
    ys = [lax.rem(y + i, 4) for i in (1, 2, 3)]
    zs = [lax.rem(z + i, 4) for i in (1, 2, 3)]
    y_peers = [index_of(z, v, core) for v in ys]
    z_peers = [index_of(v, y, core) for v in zs]
    greet([sibling] + y_peers + z_peers)
    net = Links(send, recv)
    go, got = net.go, lambda ref, r: net.got(ref, r, sibling)
    along_y, along_z = (y, ys, y_peers), (z, zs, z_peers)

    for c in range(2):
        go(even_in.at[c, 1 - core], pair_e.at[c], c * FLOWS, c * FLOWS, sibling)
        go(odd_in.at[c, 1 - core], pair_o.at[c], c * FLOWS + 1, c * FLOWS + 1, sibling)

    def flows(c):
        b = c * FLOWS
        return (
            (even_in.at[c], pair_e.at[c], half_e.at[c], relay_e.at[c], near_e.at[c], quarter_e.at[c], second_e.at[c],
             along_y, along_z, b, b + 2, b + 14),
            (odd_in.at[c], pair_o.at[c], half_o.at[c], relay_o.at[c], near_o.at[c], quarter_o.at[c], second_o.at[c],
             along_z, along_y, b + 1, b + 8, b + 17),
        )

    for c in range(2):
        for src, pair, half, relay, near, _, _, (_, others, peers), _, s0, s1, _ in flows(c):
            plus, opposite, minus = others
            got(pair, s0)

            def add(j, _):
                half[j] = (src[core, j].astype(f32) + pair[j].astype(f32)).astype(bf16)
                return 0

            lax.fori_loop(0, 4, add, 0)
            first, last = HALVES
            go(half.at[opposite, :, first], relay.at[0], s1, s1, peers[0])
            go(half.at[opposite, :, last], relay.at[1], s1 + 1, s1 + 1, peers[2])
            go(half.at[plus, :, last], near.at[0], s1 + 2, s1 + 2, peers[0])
            go(half.at[minus, :, first], near.at[1], s1 + 3, s1 + 3, peers[2])
    for c in range(2):
        for _, _, half, relay, near, _, _, (_, others, peers), _, _, s1, _ in flows(c):
            plus, opposite, minus = others
            for j, (to, rows, peer) in enumerate(((plus, HALVES[0], peers[0]), (minus, HALVES[1], peers[2]))):
                got(relay.at[j], s1 + j)
                half[to, :, rows] = (half[to, :, rows].astype(f32) + relay[j].astype(f32)).astype(bf16)
                go(half.at[to, :, rows], near.at[2 + j], s1 + 4 + j, s1 + 4 + j, peer)
    for c in range(2):
        for _, _, half, _, near, quarter, second, (own, _, _), (_, others, peers), _, s1, s2 in flows(c):
            for i in (2, 3, 4, 5):
                got(near.at[i - 2], s1 + i)
            for rows, i, j in ((HALVES[0], 1, 2), (HALVES[1], 0, 3)):
                quarter[:, rows] = (
                    half[own, :, rows].astype(f32) + near[i].astype(f32) + near[j].astype(f32)
                ).astype(bf16)
            for i in range(3):
                go(quarter.at[others[i]], second.at[2 - i], s2 + i, s2 + 2 - i, peers[i])
    a1, b1, a2, b2, sa, sb = 20, 23, 26, 30, 34, 38
    for c in range(2):
        base = c * FLOWS
        sums = []
        for _, _, _, _, _, quarter, second, _, (own, _, _), _, _, s2 in flows(c):
            for i in range(3):
                got(second.at[i], s2 + i)
            total = quarter[own].astype(f32)
            for i in range(3):
                total = total + second[i].astype(f32)
            sums.append(total)
        turned = jnp.concatenate([sums[0][:64], sums[1][:64]], axis=0).T
        for half, gath in enumerate((gath_a.at[c, core, z, y], gath_b.at[c, core, y, z])):
            gath[:64] = turned[half * 64 : half * 64 + 64].astype(bf16)
            gath[64:] = sums[half][64:].astype(bf16)
        for i in range(3):
            block = gath_a.at[c, core, z, y]
            go(block, block, base + a1 + i, base + a1 + 2 - i, y_peers[i])
            block = gath_b.at[c, core, y, z]
            go(block, block, base + b1 + i, base + b1 + 2 - i, z_peers[i])

    def gathers(c):
        base = c * FLOWS
        return (
            (gath_a.at[c], z, zs, z_peers, base + a2, base + sa, base + a1, ys),
            (gath_b.at[c], y, ys, y_peers, base + b2, base + sb, base + b1, zs),
        )

    for c in range(2):
        for gath, own, others, peers, s, f, before, fast in gathers(c):
            for i in range(3):
                got(gath.at[core, own, fast[i]], before + i)
            row = gath.at[core, own]
            go(row, row, s, s, peers[0])
            go(row, row, s + 1, s + 1, peers[2])
            go(row, row, f, f, sibling)
    for c in range(2):
        for gath, own, others, peers, s, f, before, fast in gathers(c):
            plus, opposite, minus = others
            got(gath.at[core, minus], s)
            part = gath.at[core, minus, :, HALVES[0]]
            go(part, part, s + 2, s + 2, peers[0])
            got(gath.at[core, plus], s + 1)
            part = gath.at[core, plus, :, HALVES[1]]
            go(part, part, s + 3, s + 3, peers[2])
            row = gath.at[core, minus]
            go(row, row, f + 1, f + 1, sibling)
            row = gath.at[core, plus]
            go(row, row, f + 2, f + 2, sibling)
    for c in range(2):
        for gath, own, others, peers, s, f, before, fast in gathers(c):
            plus, opposite, minus = others
            got(gath.at[core, opposite, :, HALVES[0]], s + 2)
            got(gath.at[core, opposite, :, HALVES[1]], s + 3)
            row = gath.at[core, opposite]
            go(row, row, f + 3, f + 3, sibling)
    for c in range(2):
        for gath, own, others, peers, s, f, before, fast in gathers(c):
            plus, opposite, minus = others
            for i, at in enumerate((own, minus, plus, opposite)):
                got(gath.at[1 - core, at], f + i)
    net.finish()


def final_kernel(queries, grad_out, w_query, w_out, gath_a, gath_b,
                 layer_out, grad_queries, grad_wq, grad_wk, grad_wv, grad_wo,
                 grad_q, attended):
    for qb in range(QB):
        core, z = qb // 4, qb % 4
        for p in range(PAIRS):
            for half in range(2):
                block = gath_a.at[:, core, z, p] if half == 0 else gath_b.at[:, core, p, z]
                rows = slice(qb * B + half * 64, qb * B + half * 64 + 64)
                attended[rows, pair_cols(p)] = block[0, :64]
                grad_q[rows, pair_cols(p)] = block[1, :64]
                out = grad_wk if core == 0 else grad_wv
                local = z * B + half * 64
                out[local : local + 32, pair_cols(p)] = block[0, 64:].astype(f32)
                out[local + 32 : local + 64, pair_cols(p)] = block[1, 64:].astype(f32)

    def rows_block(i, _):
        rows = block_rows(i)
        layer_out[rows, :] = (queries[rows, :].astype(f32) + dot(attended[rows, :], w_out[...])).astype(bf16)
        grad_queries[rows, :] = (grad_out[rows, :].astype(f32) + dot(grad_q[rows, :], w_query[...], NT)).astype(bf16)
        return 0

    lax.fori_loop(0, 8, rows_block, 0)
    for j in range(4):
        cols = pair_cols(j)
        grad_wq[cols, :] = dot(queries[:, cols], grad_q[...], TN)
        grad_wo[cols, :] = dot(attended[:, cols], grad_out[...], TN)


def shaped(*shape, dtype=f32):
    return jax.ShapeDtypeStruct(shape, dtype)


VMEM = pl.BlockSpec(memory_space=pltpu.VMEM)
ANY = pl.BlockSpec(memory_space=pl.ANY)
DMA = pltpu.SemaphoreType.DMA


def scratch(*shape, dtype=bf16):
    return pltpu.VMEM(shape, dtype)


def call(kernel, args, outs, scratch_shapes, collective=None, any_in=(), any_out=()):
    params = {"vmem_limit_bytes": VMEM_LIMIT}
    if collective is not None:
        params |= {"collective_id": collective, "has_side_effects": True}
    return pl.pallas_call(
        kernel,
        out_shape=outs,
        in_specs=[ANY if i in any_in else VMEM for i in range(len(args))],
        out_specs=tuple(ANY if i in any_out else VMEM for i in range(len(outs))),
        scratch_shapes=scratch_shapes,
        compiler_params=pltpu.CompilerParams(**params),
        name=kernel.__name__,
    )(*args)


def on_device(queries_in, hits_in, w_query, w_key, w_value, w_out, mask_list, grad_out):
    full, weight = scratch(N, D), scratch(D, D)
    turned = scratch(HB, D, B)
    spread = scratch(PAIRS, 2 * B, B)
    lists = [pltpu.SMEM((QB, HB + 1), jnp.int32), pltpu.SMEM((QB,), jnp.int32)]
    q, k, v, natt_e, natt_o, stats_own = call(
        forward_kernel,
        (queries_in, hits_in, w_query, w_key, w_value, grad_out, w_out, mask_list),
        (
            shaped(N, D, dtype=bf16), shaped(N, D, dtype=bf16), shaped(N, D, dtype=bf16),
            shaped(2, 4, 4, 64, B, dtype=bf16), shaped(2, 4, 4, 64, B, dtype=bf16), shaped(QB, 16, B),
        ),
        [
            full, full, weight, weight, weight, full, weight, full, full, full,
            turned, turned, spread, scratch(PAIRS, B, B, dtype=f32),
            scratch(PAIRS, 1, 2 * B, dtype=f32), scratch(PAIRS, 1, 2 * B, dtype=f32),
        ] + lists + [DMA((7,)), DMA((3,))],
        any_in=range(7),
        any_out=range(3),
    )
    two = scratch(2, 16, B, dtype=f32)
    three = scratch(3, 2, 16, B, dtype=f32)
    stats, kt, hits_t, gatt = call(
        softmax_kernel,
        (stats_own, k, hits_in, grad_out, w_out),
        (
            shaped(QB, 16, B), shaped(HB, D, B, dtype=bf16), shaped(HB, D, B, dtype=bf16),
            shaped(N, D, dtype=bf16),
        ),
        [
            scratch(4, 16, B, dtype=f32), two, two, three, three, two, two, three, three,
            full, full, full, weight, turned, turned, full, DMA((14,)), DMA((14,)), DMA((4,)), DMA((3,)),
        ],
        collective=0,
        any_in=(1, 2, 3, 4),
        any_out=(1, 2, 3),
    )
    even, odd, grad_hits = call(
        backward_kernel,
        (q, k, v, kt, gatt, stats, stats_own, natt_e, natt_o, hits_t, w_key, w_value, mask_list),
        (shaped(2, 2, 4, 4, 96, B, dtype=bf16), shaped(2, 2, 4, 4, 96, B, dtype=bf16), shaped(N, D, dtype=bf16)),
        [
            turned, weight, weight, scratch(N, D, dtype=f32), scratch(N, D, dtype=f32), full, full,
            spread, spread, scratch(PAIRS, B, B, dtype=f32),
        ] + lists + [DMA((3,))],
        any_in=(9, 10, 11),
    )
    stages = []
    for lead in ((2, 4, 4, 96), (2, 4, 4, 96), (2, 2, 4, 48), (2, 4, 4, 48), (2, 4, 96), (2, 3, 96)):
        stages += [scratch(*lead, B)] * 2
    gath_a, gath_b = call(
        total_kernel,
        (even, odd),
        (shaped(2, 2, 4, 4, 96, B, dtype=bf16), shaped(2, 2, 4, 4, 96, B, dtype=bf16)),
        stages + [DMA((2 * FLOWS,)), DMA((2 * FLOWS,))],
        collective=1,
    )
    layer_out, grad_queries, grad_wq, grad_wk, grad_wv, grad_wo = call(
        final_kernel,
        (queries_in, grad_out, w_query, w_out, gath_a, gath_b),
        (
            shaped(N, D, dtype=bf16), shaped(N, D, dtype=bf16),
            shaped(D, D), shaped(D, D), shaped(D, D), shaped(D, D),
        ),
        [full, full],
    )
    return (layer_out, grad_queries, grad_hits, grad_wq, grad_wk, grad_wv, grad_wo)


def solution(mesh):
    per_event = P("event", None)
    per_region = P(("event", "region"), None)
    return jax.shard_map(
        on_device,
        mesh=mesh,
        in_specs=(per_event, per_region, P(), P(), P(), P(), per_event, per_event),
        out_specs=(per_event, per_event, per_region, per_event, per_event, per_event, per_event),
        check_vma=False,
    )
```

time: 140 us -> 101 us (0.72)
  the two profiles are of different devices: /device:TPU:3 before, /device:TPU:1 now
where the time goes in v2:
time: 101 us; the launch traced here: 100 us
  Pallas kernels  99.6 us (99%)
    pallas_call x5, Pallas kernels, call(): pl.pallas_call(kernel, out_shape=outs, in_specs=[ANY if i in any_in else...  99.6 us

profile of v2, /device:TPU:1, one launch (start us, length us, event | category | flops | bytes accessed | tf_op | source)
XLA Modules:
  0.0 100.3 jit_solution(16790193310500388446)
XLA Ops:
  0.6 15.1 %forward_kernel.1 = (bf16[1024,512]{1,0:T(8,128)(2,1)}, bf16[1024,512]{1,0:T(8,128)(2,1)}, bf16[1024,512]{1,0:T(8,128)(2,1)}, bf16[2,4,4,64,128]{4,3,2,1,0:T(8,1...) custom-call(bf16[1024,512]{1,0:T(8,128)(2,1)} %queries.1, bf16[1024,512]{1,0:T(8,128)(2,1)} %hits_h.3, ...), custom_call_target="tpu_custom_call" | custom-call | tf_op jit(solution)/shard_map/forward_kernel/pallas_call | solution.py:574
  15.7 20.5 %softmax_kernel.1 = (f32[8,16,128]{2,1,0:T(8,128)}, bf16[8,512,128]{2,1,0:T(8,128)(2,1)}, bf16[8,512,128]{2,1,0:T(8,128)(2,1)}, bf16[1024,512]{1,0:T(8,128)(2,1)}) custom-call(f32[8,16,128]{2,1,0:T(8,128)} %get-tuple-element.31.stats_in.stats_own, bf16[1024,512]{1,0:T(8,128)(2,1)} %get-tuple-element.29.k_h.k, bf16[1024,512]{1,0:T(8,128)(2,1)} %hits_h.3, ...), custom_call_target="tpu_custom_call" | custom-call | tf_op jit(solution)/shard_map/softmax_kernel/pallas_call | solution.py:574
  36.3 15.2 %backward_kernel.1 = (bf16[2,2,4,4,96,128]{5,4,3,2,1,0:T(8,128)(2,1)}, bf16[2,2,4,4,96,128]{5,4,3,2,1,0:T(8,128)(2,1)}, bf16[1024,512]{1,0:T(8,128)(2,1)}) custom-call(bf16[1024,512]{1,0:T(8,128)(2,1)} %get-tuple-element.28.q, bf16[1024,512]{1,0:T(8,128)(2,1)} %get-tuple-element.29.k_h.k, bf16[1024,512]{1,0:T(8,128)(2,1)} %get-tuple-element.30.v, ...), custom_call_target="tpu_custom_call" | custom-call | tf_op jit(solution)/shard_map/backward_kernel/pallas_call | solution.py:574
  51.5 39.8 %total_kernel.1 = (bf16[2,2,4,4,96,128]{5,4,3,2,1,0:T(8,128)(2,1)}, bf16[2,2,4,4,96,128]{5,4,3,2,1,0:T(8,128)(2,1)}) custom-call(bf16[2,2,4,4,96,128]{5,4,3,2,1,0:T(8,128)(2,1)} %get-tuple-element.38.even_in, bf16[2,2,4,4,96,128]{5,4,3,2,1,0:T(8,128)(2,1)} %get-tuple-element.39.odd_in), custom_call_target="tpu_custom_call" | custom-call | tf_op jit(solution)/shard_map/total_kernel/pallas_call | solution.py:574
  91.3 9.0 %final_kernel.1 = (bf16[1024,512]{1,0:T(8,128)(2,1)}, bf16[1024,512]{1,0:T(8,128)(2,1)}, f32[512,512]{1,0:T(8,128)}, f32[512,512]{1,0:T(8,128)}, f32[512,512]{1,0:T(8,128)}, /*index=5*/f32[512,512]{1,0:T(8,128)}) custom-call(bf16[1024,512]{1,0:T(8,128)(2,1)} %queries.1, bf16[1024,512]{1,0:T(8,128)(2,1)} %grad_out.1, bf16[512,512]{1,0:T(8,128)(2,1)} %w_query.1, ...), custom_call_target="tpu_custom_call" | custom-call | tf_op jit(solution)/shard_map/final_kernel/pallas_call | solution.py:574

commit v3 on v2

v3 whole, which is shorter than its diff:
```python
import jax
import jax.numpy as jnp
from jax import lax
from jax.experimental import pallas as pl
from jax.experimental.pallas import tpu as pltpu
from jax.sharding import PartitionSpec as P

f32 = jnp.float32
bf16 = jnp.bfloat16
HEADS = 8
PAIRS = 4
B = 128
QB = 8
HB = 8
D = 512
N = 1024
SCALE = 0.125
NEG = -1e30
MIB = 1024 * 1024
VMEM_LIMIT = 28 * MIB
FORWARD_LIMIT = 53 * MIB
MESH = pl.DeviceIdType.MESH
NN = (((1,), (0,)), ((), ()))
NT = (((1,), (1,)), ((), ()))
TN = (((0,), (0,)), ((), ()))


def dot(a, b, dims=NN):
    return lax.dot_general(a, b, dims, preferred_element_type=f32)


def transposed(block):
    return block.astype(f32).T.astype(block.dtype)


def pair_cols(p):
    return slice(p * B, (p + 1) * B)


def block_rows(i):
    return pl.ds(pl.multiple_of(i * B, B), B)


def list_blocks(mask_ref, lists, counts):
    first = lax.axis_index("region") * HB
    slot = mask_ref[...] - first
    inside = (slot >= 0) & (slot < HB)
    weight = jnp.where(inside, jnp.left_shift(1, jnp.clip(slot, 0, HB - 1)), 0).astype(f32)
    for qb in range(QB):
        bits = jnp.sum(weight[qb : qb + 1, :]).astype(jnp.int32)
        count = jnp.int32(0)
        for hb in range(HB):
            lists[qb, count] = hb
            count = count + (jnp.right_shift(bits, hb) & 1)
        counts[qb] = count


def over_listed(lists, counts, qb, body):
    count = counts[qb]

    def two(i, _):
        body([lists[qb, 2 * i], lists[qb, 2 * i + 1]])
        return 0

    lax.fori_loop(0, count // 2, two, 0)

    @pl.when(lax.rem(count, 2) == 1)
    def _():
        body([lists[qb, count - 1]])


def gathered_rows(ref, blocks, cols):
    return jnp.concatenate([ref[block_rows(b), cols] for b in blocks], axis=0)


def gathered_cols(ref, blocks, rows):
    return jnp.concatenate([ref[b, rows, :] for b in blocks], axis=1)


def lane_masks():
    lane = lax.broadcasted_iota(jnp.int32, (1, B), 1)
    even = jnp.where(lane < 64, 1.0, 0.0)
    return even.astype(bf16), (1.0 - even).astype(bf16)


def spread_heads(rows, p, out, masks):
    block = rows[:, pair_cols(p)]
    out[p, :B] = block * masks[0]
    out[p, B:] = block * masks[1]


def loads(pairs, sems):
    copies = [pltpu.make_async_copy(src, dst, sems.at[i]) for i, (src, dst) in enumerate(pairs)]
    for c in copies:
        c.start()
    return copies


def forward_kernel(queries_h, hits_h, w_query_h, w_key_h, w_value_h, grad_out_h, w_out_h, mask_ref,
                   q_h, k_h, v_h, natt_e, natt_o, stats,
                   queries, hits, w_query, w_key, w_value, grad_out, w_out, q, k, v,
                   gatt_t, heads_q, acc, peak, total, lists, counts, sems_in, sems_out):
    ins = loads(
        ((hits_h, hits), (w_value_h, w_value), (w_key_h, w_key), (queries_h, queries),
         (w_query_h, w_query), (grad_out_h, grad_out), (w_out_h, w_out)), sems_in)
    list_blocks(mask_ref, lists, counts)
    masks = lane_masks()

    def project(src, weight, out, scale=None):
        def part(i, _):
            rows = pl.ds(pl.multiple_of(i * 256, 256), 256)
            x = dot(src[rows, :], weight[...])
            out[rows, :] = (x if scale is None else x * scale).astype(bf16)
            return 0

        lax.fori_loop(0, 4, part, 0)

    ins[0].wait()
    ins[1].wait()
    project(hits, w_value, v)
    saves = loads(((v, v_h),), sems_out)

    ins[2].wait()
    project(hits, w_key, k)
    saves += loads(((k, k_h),), sems_out.at[pl.ds(1, 1)])
    ins[3].wait()
    ins[4].wait()
    project(queries, w_query, q, SCALE)
    saves += loads(((q, q_h),), sems_out.at[pl.ds(2, 1)])
    ins[5].wait()
    ins[6].wait()

    def grads(i, _):
        x = dot(w_out[...], grad_out[pl.ds(pl.multiple_of(i * 256, 256), 256), :], NT).astype(bf16)
        gatt_t[2 * i] = x[:, :B]
        gatt_t[2 * i + 1] = x[:, B:]
        return 0

    lax.fori_loop(0, 4, grads, 0)

    def query_block(qb, _):
        rows = q[block_rows(qb), :]
        for p in range(PAIRS):
            spread_heads(rows, p, heads_q, masks)
        peak[...] = jnp.full(peak.shape, NEG, f32)
        total[...] = jnp.zeros(total.shape, f32)
        acc[...] = jnp.zeros(acc.shape, f32)

        def body(blocks):
            ps = range(PAIRS)
            scores = [dot(gathered_rows(k, blocks, pair_cols(p)), heads_q[p], NT) for p in ps]
            old = [peak[p] for p in ps]
            new = [jnp.maximum(o, jnp.max(s, axis=0, keepdims=True)) for o, s in zip(old, scores)]
            shrink = [jnp.exp(o - n) for o, n in zip(old, new)]
            expo = [jnp.exp(s - n) for s, n in zip(scores, new)]
            numer = [dot(gathered_rows(v, blocks, pair_cols(p)), expo[p].astype(bf16), TN) for p in ps]
            for p in ps:
                peak[p] = new[p]
                total[p] = total[p] * shrink[p] + jnp.sum(expo[p], axis=0, keepdims=True)
                acc[p, :64] = acc[p, :64] * shrink[p][:, :B] + numer[p][:64, :B]
                acc[p, 64:] = acc[p, 64:] * shrink[p][:, B:] + numer[p][64:, B:]

        over_listed(lists, counts, qb, body)
        core, z = qb // 4, lax.rem(qb, 4)
        for p in range(PAIRS):
            some = total[p] > 0.0
            safe = jnp.where(some, total[p], 1.0)
            log_total = jnp.where(some, peak[p] + jnp.log(safe), NEG)
            inverse = 1.0 / safe
            for half, out in enumerate((natt_e.at[core, p, z], natt_o.at[core, z, p])):
                lanes = slice(half * B, (half + 1) * B)
                rows = slice(half * 64, half * 64 + 64)
                part = acc[p, rows] * inverse[:, lanes]
                out[...] = part.astype(bf16)
                grads = gatt_t[qb, p * B + half * 64 : p * B + half * 64 + 64, :].astype(f32)
                h = 2 * p + half
                stats[qb, h : h + 1, :] = log_total[:, lanes]
                stats[qb, 8 + h : 9 + h, :] = jnp.sum(part * grads, axis=0, keepdims=True)
        return 0

    lax.fori_loop(0, QB, query_block, 0)
    for c in saves:
        c.wait()


def place():
    r = lax.axis_index("region")
    return r // 8, lax.rem(r // 2, 4), lax.rem(r, 2)


def index_of(z, y, core):
    return (z * 4 + y) * 2 + core


def remote(src, dst, send, recv, peer):
    return pltpu.make_async_remote_copy(
        src_ref=src, dst_ref=dst, send_sem=send, recv_sem=recv,
        device_id={"region": peer}, device_id_type=MESH,
    )


def greet(peers):
    barrier = pltpu.get_barrier_semaphore()
    for peer in peers:
        pl.semaphore_signal(barrier, inc=1, device_id={"region": peer}, device_id_type=MESH)
    pl.semaphore_wait(barrier, len(peers))


class Links:
    def __init__(self, send, recv):
        self.send, self.recv, self.sent = send, recv, []

    def go(self, src, dst, s, r, peer):
        d = remote(src, dst, self.send.at[s], self.recv.at[r], peer)
        d.start()
        self.sent.append(d)

    def got(self, ref, r, peer):
        remote(ref, ref, self.send.at[r], self.recv.at[r], peer).wait_recv()

    def finish(self):
        for d in self.sent:
            d.wait_send()


def merge(parts):
    peak = parts[0][:, :8]
    for part in parts[1:]:
        peak = jnp.maximum(peak, part[:, :8])
    total = None
    for part in parts:
        w = jnp.exp(part[:, :8] - peak)
        total = w if total is None else total + w
    log_total = peak + jnp.log(total)
    delta = None
    for part in parts:
        d = part[:, 8:] * jnp.exp(part[:, :8] - log_total)
        delta = d if delta is None else delta + d
    return jnp.concatenate([log_total, delta], axis=1)


def softmax_kernel(stats_in, hits, grad_out, w_out,
                   stats, hits_t, gatt,
                   pair, half_a, half_b, got_a1, got_b1, mid_a, mid_b, got_a2, got_b2,
                   send, recv):
    z, y, core = place()
    sibling = index_of(z, y, 1 - core)
    ys = [lax.rem(y + i, 4) for i in (1, 2, 3)]
    zs = [lax.rem(z + i, 4) for i in (1, 2, 3)]
    y_peers = [index_of(z, v, core) for v in ys]
    z_peers = [index_of(v, y, core) for v in zs]
    greet([sibling] + y_peers + z_peers)
    net = Links(send, recv)
    theirs, mine = pl.ds(4 * (1 - core), 4), 4 * core
    net.go(stats_in.at[theirs], pair, 0, 0, sibling)
    def grad_att(i):
        rows = slice(i * 256, i * 256 + 256)
        gatt[rows, :] = dot(grad_out[rows, :], w_out[...], NT).astype(bf16)

    def turn(src, dst, first, count):
        def one(i, _):
            dst[i] = transposed(src[block_rows(i), :])
            return 0

        lax.fori_loop(first, first + count, one, 0)

    net.got(pair, 0, sibling)
    half_a[...] = merge([stats_in[pl.ds(mine, 2)], pair[:2]])
    half_b[...] = merge([stats_in[pl.ds(mine + 2, 2)], pair[2:]])
    for i in range(3):
        net.go(half_a, got_a1.at[2 - i], 1 + i, 1 + 2 - i, y_peers[i])
        net.go(half_b, got_b1.at[2 - i], 4 + i, 4 + 2 - i, z_peers[i])
    grad_att(0)
    grad_att(1)
    for i in range(3):
        net.got(got_a1.at[i], 1 + i, y_peers[i])
        net.got(got_b1.at[i], 4 + i, z_peers[i])
    mid_a[...] = merge([half_a[...], got_a1[0], got_a1[1], got_a1[2]])
    mid_b[...] = merge([half_b[...], got_b1[0], got_b1[1], got_b1[2]])
    for i in range(3):
        net.go(mid_a, got_a2.at[2 - i], 7 + i, 7 + 2 - i, z_peers[i])
        net.go(mid_b, got_b2.at[2 - i], 10 + i, 10 + 2 - i, y_peers[i])
    grad_att(2)
    grad_att(3)
    turn(hits, hits_t, 0, 4)
    for i in range(3):
        net.got(got_a2.at[i], 7 + i, z_peers[i])
        net.got(got_b2.at[i], 10 + i, y_peers[i])
    stats[pl.ds(mine, 2)] = merge([mid_a[...], got_a2[0], got_a2[1], got_a2[2]])
    stats[pl.ds(mine + 2, 2)] = merge([mid_b[...], got_b2[0], got_b2[1], got_b2[2]])
    here = stats.at[pl.ds(mine, 4)]
    net.go(here, here, 13, 13, sibling)
    turn(hits, hits_t, 4, 4)
    net.got(stats.at[theirs], 13, sibling)
    net.finish()


def backward_kernel(q, k, v, gatt, stats, stats_own, natt_e, natt_o, mask_ref,
                    even_out, odd_out, dkb, dvb,
                    dk, dv, heads_q, heads_g, acc, lists, counts):
    list_blocks(mask_ref, lists, counts)
    masks = lane_masks()
    dk[...] = jnp.zeros(dk.shape, f32)
    dv[...] = jnp.zeros(dv.shape, f32)

    def query_block(qb, _):
        core, z = qb // 4, lax.rem(qb, 4)
        rows, grads = q[block_rows(qb), :], gatt[block_rows(qb), :]
        for p in range(PAIRS):
            spread_heads(rows, p, heads_q, masks)
            spread_heads(grads, p, heads_g, masks)
        acc[...] = jnp.zeros(acc.shape, f32)

        def stat_row(p, base):
            h = base + 2 * p
            return jnp.concatenate([stats[qb, h : h + 1, :], stats[qb, h + 1 : h + 2, :]], axis=1)

        def body(blocks):
            ps = range(PAIRS)
            keys = [gathered_rows(k, blocks, pair_cols(p)) for p in ps]
            vals = [gathered_rows(v, blocks, pair_cols(p)) for p in ps]
            scores = [dot(keys[p], heads_q[p], NT) for p in ps]
            dps = [dot(vals[p], heads_g[p], NT) for p in ps]
            probs = [jnp.exp(scores[p] - stat_row(p, 0)) for p in ps]
            ds = [(probs[p] * (dps[p] - stat_row(p, 8))).astype(bf16) for p in ps]
            dvs = [dot(probs[p].astype(bf16), heads_g[p]) for p in ps]
            dks = [dot(ds[p], heads_q[p]) for p in ps]
            dqs = [dot(keys[p], ds[p], TN) for p in ps]
            for p in ps:
                for j, b in enumerate(blocks):
                    part = slice(j * B, (j + 1) * B)
                    dv[block_rows(b), pair_cols(p)] += dvs[p][part]
                    dk[block_rows(b), pair_cols(p)] += dks[p][part]
                acc[p, :64] = acc[p, :64] + dqs[p][:64, :B]
                acc[p, 64:] = acc[p, 64:] + dqs[p][64:, B:]

        over_listed(lists, counts, qb, body)
        for p in range(PAIRS):
            for half, (out, natt) in enumerate(
                ((even_out.at[:, core, p, z], natt_e.at[core, p, z]), (odd_out.at[:, core, z, p], natt_o.at[core, z, p]))
            ):
                h = 2 * p + half
                weight = jnp.exp(stats_own[qb, h : h + 1, :] - stats[qb, h : h + 1, :])
                out[0] = (natt[...].astype(f32) * weight).astype(bf16)
                out[1] = (acc[p, half * 64 : half * 64 + 64] * SCALE).astype(bf16)
        return 0

    lax.fori_loop(0, QB, query_block, 0)
    dkb[...] = dk[...].astype(bf16)
    dvb[...] = dv[...].astype(bf16)


CHUNKS = 3
FLOWS = 34
FAR_FIRST = (1, 0, 2)


def total_kernel(even_in, odd_in, dkb, dvb, hits_t, w_key, w_value, queries, grad_out, w_out,
                 gath_a, gath_b, grad_hits, layer_out, grad_wo,
                 attended, weight_e, weight_o, pair_e, pair_o, half_e, half_o, first_e, first_o, quarter_e, quarter_o, second_e, second_o,
                 send, recv):
    z, y, core = place()
    sibling = index_of(z, y, 1 - core)
    ys = [lax.rem(y + i, 4) for i in (1, 2, 3)]
    zs = [lax.rem(z + i, 4) for i in (1, 2, 3)]
    y_peers = [index_of(z, v, core) for v in ys]
    z_peers = [index_of(v, y, core) for v in zs]
    greet([sibling] + y_peers + z_peers)
    net = Links(send, recv)
    go, got = net.go, lambda ref, r: net.got(ref, r, sibling)
    along_y, along_z = (y, ys, y_peers), (z, zs, z_peers)

    sources = [(even_in.at[c], odd_in.at[c]) for c in range(2)] + [(weight_e, weight_o)]

    def send_pair(c):
        for i, (src, pair) in enumerate(zip(sources[c], (pair_e, pair_o))):
            go(src.at[1 - core], pair.at[c], c * FLOWS + i, c * FLOWS + i, sibling)

    def weight_grads(c):
        left = jnp.concatenate([hits_t[i] for i in range(HB)], axis=1)
        for which, grad in enumerate((dkb, dvb)):
            for side in range(2):
                part = dot(left, grad[:, side * 256 : side * 256 + 256]).astype(bf16)
                for p in (2 * side, 2 * side + 1):
                    for v in range(4):
                        tile = part[v * B : (v + 1) * B, pair_cols(p - 2 * side)]
                        weight_e[which, p, v] = tile[:64]
                        weight_o[which, v, p] = tile[64:]
        send_pair(c)

    def hit_grads(half):
        for i in range(2 * half, 2 * half + 2):
            rows = slice(i * 256, i * 256 + 256)
            x = dot(dkb[rows, :], w_key[...], NT) + dot(dvb[rows, :], w_value[...], NT)
            grad_hits[rows, :] = x.astype(bf16)

    def attended_products(c):
        for qb in range(QB):
            for p in range(PAIRS):
                parts = gath_a[c, qb // 4, qb % 4, p], gath_b[c, qb // 4, p, qb % 4]
                for half, block in enumerate(parts):
                    row = qb * B + half * 64
                    attended[row : row + 64, pair_cols(p)] = block
        for i in range(4):
            rows = slice(i * 256, i * 256 + 256)
            layer_out[rows, :] = (queries[rows, :].astype(f32) + dot(attended[rows, :], w_out[...])).astype(bf16)
        for i in range(2):
            cols = slice(i * 256, i * 256 + 256)
            grad_wo[cols, :] = dot(attended[:, cols], grad_out[...], TN)

    def flows(c):
        b = c * FLOWS
        return (
            (sources[c][0].at[core], pair_e.at[c], half_e.at[c], first_e.at[c], quarter_e.at[c], second_e.at[c],
             along_y, along_z, b, b + 2, b + 8),
            (sources[c][1].at[core], pair_o.at[c], half_o.at[c], first_o.at[c], quarter_o.at[c], second_o.at[c],
             along_z, along_y, b + 1, b + 5, b + 11),
        )

    def add_cores(c):
        for src, pair, half, first, _, _, (_, others, peers), _, s0, s1, _ in flows(c):
            got(pair, s0)
            for i in FAR_FIRST:
                half[i] = src[others[i]] + pair[others[i]]
                go(half.at[i], first.at[2 - i], s1 + i, s1 + 2 - i, peers[i])

    def add_first(c):
        for src, pair, _, first, quarter, second, (own, _, _), (_, others, peers), _, s1, s2 in flows(c):
            total = src[own].astype(f32) + pair[own].astype(f32)
            for i in range(3):
                got(first.at[i], s1 + i)
                total = total + first[i].astype(f32)
            quarter[...] = total.astype(bf16)
            for i in FAR_FIRST:
                go(quarter.at[others[i]], second.at[2 - i], s2 + i, s2 + 2 - i, peers[i])

    a1, b1, a2, b2, sa, sb = 14, 17, 20, 23, 26, 30

    def add_second(c):
        base = c * FLOWS
        sums = []
        for _, _, _, _, quarter, second, _, (own, _, _), _, _, s2 in flows(c):
            total = quarter[own].astype(f32)
            for i in range(3):
                got(second.at[i], s2 + i)
                total = total + second[i].astype(f32)
            sums.append(total)
        if c < 2:
            turned = jnp.concatenate(sums, axis=0).T
            sums = [turned[:64], turned[64:]]
        blocks = gath_a.at[c, core, z, y], gath_b.at[c, core, y, z]
        for block, part in zip(blocks, sums):
            block[...] = part.astype(bf16)
        for i in FAR_FIRST:
            go(blocks[0], blocks[0], base + a1 + i, base + a1 + 2 - i, y_peers[i])
            go(blocks[1], blocks[1], base + b1 + i, base + b1 + 2 - i, z_peers[i])

    def gathers(c):
        base = c * FLOWS
        return (
            (gath_a.at[c], z, zs, z_peers, base + a2, base + sa, base + a1, ys),
            (gath_b.at[c], y, ys, y_peers, base + b2, base + sb, base + b1, zs),
        )

    def pass_row(c):
        for gath, own, others, peers, s, f, before, fast in gathers(c):
            for i in range(3):
                got(gath.at[core, own, fast[i]], before + i)
            row = gath.at[core, own]
            for i in FAR_FIRST:
                go(row, row, s + i, s + 2 - i, peers[i])
            go(row, row, f + 3, f + 3, sibling)

    def pass_sibling(c):
        for gath, own, others, peers, s, f, before, fast in gathers(c):
            for i in (0, 2, 1):
                row = gath.at[core, others[i]]
                got(row, s + i)
                go(row, row, f + i, f + i, sibling)

    def from_sibling(c):
        for gath, own, others, peers, s, f, before, fast in gathers(c):
            for i in range(3):
                got(gath.at[1 - core, others[i]], f + i)
            got(gath.at[1 - core, own], f + 3)

    for step, c in (
        (send_pair, 0), (send_pair, 1), (add_cores, 0), (add_cores, 1), (weight_grads, 2), (add_first, 0),
        (add_first, 1), (add_cores, 2), (hit_grads, 0), (add_second, 0), (add_second, 1), (hit_grads, 1),
        (add_first, 2), (pass_row, 0), (pass_row, 1), (add_second, 2), (pass_sibling, 0), (pass_sibling, 1),
        (pass_row, 2), (from_sibling, 0), (attended_products, 0), (pass_sibling, 2), (from_sibling, 1),
        (from_sibling, 2),
    ):
        step(c)
    net.finish()


def final_kernel(queries, grad_out, w_query, gath_a, gath_b, grad_hits_in, layer_in, grad_wo_in, *refs):
    outs, bufs = refs[:7], refs[7:11]
    grad_q, sems = refs[11:]
    grad_queries, grad_wq, grad_wk, grad_wv = bufs
    ready = (layer_in, grad_queries, grad_hits_in, grad_wq, grad_wk, grad_wv, grad_wo_in)
    saves = []

    def save(i):
        c = pltpu.make_async_copy(ready[i], outs[i], sems.at[i])
        c.start()
        saves.append(c)

    for i in (0, 2, 6):
        save(i)

    def blocks(chunk, qb, p):
        core, z = qb // 4, qb % 4
        return gath_a[chunk, core, z, p], gath_b[chunk, core, p, z]

    def place_blocks(chunk, qb, p, out, row):
        for half, block in enumerate(blocks(chunk, qb, p)):
            out[row + half * 64 : row + half * 64 + 64, pair_cols(p)] = block.astype(out.dtype)

    for qb in range(QB):
        for p in range(PAIRS):
            place_blocks(2, qb, p, grad_wk if qb < 4 else grad_wv, (qb % 4) * B)
            place_blocks(1, qb, p, grad_q, qb * B)
        if qb == 3:
            save(4)
    save(5)

    for j in range(2):
        cols = slice(j * 256, j * 256 + 256)
        grad_wq[cols, :] = dot(queries[:, cols], grad_q[...], TN)
    save(3)
    for i in range(4):
        rows = slice(i * 256, i * 256 + 256)
        grad_queries[rows, :] = (grad_out[rows, :].astype(f32) + dot(grad_q[rows, :], w_query[...], NT)).astype(bf16)
    save(1)
    for c in saves:
        c.wait()


def shaped(*shape, dtype=f32):
    return jax.ShapeDtypeStruct(shape, dtype)


VMEM = pl.BlockSpec(memory_space=pltpu.VMEM)
ANY = pl.BlockSpec(memory_space=pl.ANY)
DMA = pltpu.SemaphoreType.DMA


def scratch(*shape, dtype=bf16):
    return pltpu.VMEM(shape, dtype)


def call(kernel, args, outs, scratch_shapes, collective=None, any_in=(), any_out=(), vmem=VMEM_LIMIT):
    params = {"vmem_limit_bytes": vmem}
    if collective is not None:
        params |= {"collective_id": collective, "has_side_effects": True}
    return pl.pallas_call(
        kernel,
        out_shape=outs,
        in_specs=[ANY if i in any_in else VMEM for i in range(len(args))],
        out_specs=tuple(ANY if i in any_out else VMEM for i in range(len(outs))),
        scratch_shapes=scratch_shapes,
        compiler_params=pltpu.CompilerParams(**params),
        name=kernel.__name__,
    )(*args)


STAGE_SHAPES = ((3, 4, 4, 64), (3, 3, 4, 64), (3, 3, 4, 64), (3, 4, 64), (3, 3, 64))


def on_device(queries_in, hits_in, w_query, w_key, w_value, w_out, mask_list, grad_out):
    full, weight = scratch(N, D), scratch(D, D)
    turned = scratch(HB, D, B)
    spread = scratch(PAIRS, 2 * B, B)
    lists = [pltpu.SMEM((QB, HB + 1), jnp.int32), pltpu.SMEM((QB,), jnp.int32)]
    q, k, v, natt_e, natt_o, stats_own = call(
        forward_kernel,
        (queries_in, hits_in, w_query, w_key, w_value, grad_out, w_out, mask_list),
        (
            shaped(N, D, dtype=bf16), shaped(N, D, dtype=bf16), shaped(N, D, dtype=bf16),
            shaped(2, 4, 4, 64, B, dtype=bf16), shaped(2, 4, 4, 64, B, dtype=bf16), shaped(QB, 16, B),
        ),
        [
            full, full, weight, weight, weight, full, weight, full, full, full,
            turned, spread, scratch(PAIRS, B, B, dtype=f32),
            scratch(PAIRS, 1, 2 * B, dtype=f32), scratch(PAIRS, 1, 2 * B, dtype=f32),
        ] + lists + [DMA((7,)), DMA((3,))],
        any_in=range(7),
        any_out=range(3),
        vmem=FORWARD_LIMIT,
    )
    two = scratch(2, 16, B, dtype=f32)
    three = scratch(3, 2, 16, B, dtype=f32)
    stats, hits_t, gatt = call(
        softmax_kernel,
        (stats_own, hits_in, grad_out, w_out),
        (
            shaped(QB, 16, B), shaped(HB, D, B, dtype=bf16),
            shaped(N, D, dtype=bf16),
        ),
        [
            scratch(4, 16, B, dtype=f32), two, two, three, three, two, two, three, three,
            DMA((14,)), DMA((14,)),
        ],
        collective=0,
        vmem=8 * MIB,
    )
    even, odd, dkb, dvb = call(
        backward_kernel,
        (q, k, v, gatt, stats, stats_own, natt_e, natt_o, mask_list),
        (
            shaped(2, 2, 4, 4, 64, B, dtype=bf16), shaped(2, 2, 4, 4, 64, B, dtype=bf16),
            shaped(N, D, dtype=bf16), shaped(N, D, dtype=bf16),
        ),
        [
            scratch(N, D, dtype=f32), scratch(N, D, dtype=f32),
            spread, spread, scratch(PAIRS, B, B, dtype=f32),
        ] + lists,
        vmem=20 * MIB,
    )
    stages = [full, scratch(2, 4, 4, 64, B), scratch(2, 4, 4, 64, B)]
    for lead in STAGE_SHAPES:
        stages += [scratch(*lead, B)] * 2
    gath_a, gath_b, grad_hits, layer_out, grad_wo = call(
        total_kernel,
        (even, odd, dkb, dvb, hits_t, w_key, w_value, queries_in, grad_out, w_out),
        (
            shaped(3, 2, 4, 4, 64, B, dtype=bf16), shaped(3, 2, 4, 4, 64, B, dtype=bf16),
            shaped(N, D, dtype=bf16), shaped(N, D, dtype=bf16), shaped(D, D),
        ),
        stages + [DMA((CHUNKS * FLOWS,)), DMA((CHUNKS * FLOWS,))],
        collective=1,
        vmem=20 * MIB,
    )
    square = scratch(D, D, dtype=f32)
    layer_out, grad_queries, grad_hits, grad_wq, grad_wk, grad_wv, grad_wo = call(
        final_kernel,
        (queries_in, grad_out, w_query, gath_a, gath_b, grad_hits, layer_out, grad_wo),
        (
            shaped(N, D, dtype=bf16), shaped(N, D, dtype=bf16), shaped(N, D, dtype=bf16),
            shaped(D, D), shaped(D, D), shaped(D, D), shaped(D, D),
        ),
        [full, square, square, square, full, DMA((7,))],
        any_in=(5, 6, 7),
        any_out=range(7),
        vmem=14 * MIB,
    )
    return (layer_out, grad_queries, grad_hits, grad_wq, grad_wk, grad_wv, grad_wo)


def solution(mesh):
    per_event = P("event", None)
    per_region = P(("event", "region"), None)
    return jax.shard_map(
        on_device,
        mesh=mesh,
        in_specs=(per_event, per_region, P(), P(), P(), P(), per_event, per_event),
        out_specs=(per_event, per_event, per_region, per_event, per_event, per_event, per_event),
        check_vma=False,
    )
```

time: 101 us -> 90.2 us (0.89)
  Pallas kernels: 99.6 us -> 87.1 us
  local copies, waits for them, and re-layouts: 0 us -> 2.06 us
    pallas_call x5, Pallas kernels: 99.6 us -> 87.1 us  [call(): pl.pallas_call(kernel, out_shape=outs, in_specs=[ANY if i in any_in else...]
    unnamed x0 -> x24, local copies, waits for them, and re-layouts: none -> 2.06 us
where the time goes in v3:
time: 90.2 us; the launch traced here: 90 us
  Pallas kernels  87.1 us (97%)
  local copies, waits for them, and re-layouts  2.06 us (2%)
    pallas_call x5, Pallas kernels, call(): pl.pallas_call(kernel, out_shape=outs, in_specs=[ANY if i in any_in else...  87.1 us
    unnamed x24, local copies, waits for them, and re-layouts  2.06 us

profile of v3, /device:TPU:1, one launch (start us, length us, event | category | flops | bytes accessed | tf_op | source)
XLA Modules:
  0.0 90.0 jit_solution(6083349425950339983)
XLA Ops:
  0.6 0.0 copy-start
  0.6 0.0 copy-start.2
  0.7 0.0 copy-start.11
  0.7 0.8 copy-done.11
  1.5 0.0 copy-start.3
  1.5 13.3 %forward_kernel.1 = (bf16[1024,512]{1,0:T(8,128)(2,1)}, bf16[1024,512]{1,0:T(8,128)(2,1)}, bf16[1024,512]{1,0:T(8,128)(2,1)}, bf16[2,4,4,64,128]{4,3,2,1,0:T(8,1...) custom-call(bf16[1024,512]{1,0:T(8,128)(2,1)} %queries.3, bf16[1024,512]{1,0:T(8,128)(2,1)} %hits.1, ...), custom_call_target="tpu_custom_call" | custom-call | tf_op jit(solution)/shard_map/forward_kernel/pallas_call | solution.py:558
  14.8 0.0 copy-start.7
  14.8 0.0 copy-start.8
  14.8 0.0 copy-start.10
  14.8 0.0 copy-done
  14.8 0.0 copy-done.2
  14.8 0.0 copy-done.3
  14.8 19.6 %softmax_kernel.1 = (f32[8,16,128]{2,1,0:T(8,128)S(1)}, bf16[8,512,128]{2,1,0:T(8,128)(2,1)S(1)}, bf16[1024,512]{1,0:T(8,128)(2,1)S(1)}) custom-call(f32[8,16,128]{2,1,0:T(8,128)S(1)} %get-tuple-element.28.stats_in.stats_own, bf16[1024,512]{1,0:T(8,128)(2,1)S(1)} %copy-done.3, bf16[1024,512]{1,0:T(8,128)(2,1)S(1)} %copy-done, bf16[512,512]{1,0:T(8,128)(2,1)S(1)} %copy-done.2), custom_call_target="tpu_custom_call" | custom-call | tf_op jit(solution)/shard_map/softmax_kernel/pallas_call | solution.py:558
  34.4 0.0 copy-done.7
  34.4 0.0 copy-done.8
  34.5 0.0 copy-done.10
  34.5 0.0 copy-start.9
  34.5 1.2 %copy-done.9 = bf16[1024,512]{1,0:T(8,128)(2,1)S(1)} copy-done((bf16[1024,512]{1,0:T(8,128)(2,1)S(1)}, bf16[1024,512]{1,0:T(8,128)(2,1)}, u32[]{:S(2)}) %copy-start.9) | copy-done | bytes 1048600
  35.7 0.0 copy-start.1
  35.7 0.0 copy-start.4
  35.7 0.0 copy-start.5
  35.7 7.5 %backward_kernel.1 = (bf16[2,2,4,4,64,128]{5,4,3,2,1,0:T(8,128)(2,1)S(1)}, bf16[2,2,4,4,64,128]{5,4,3,2,1,0:T(8,128)(2,1)S(1)}, bf16[1024,512]{1,0:T(8,128)(2,1)S(1)}, bf16[1024,512]{1,0:T(8,128)(2,1)S(1)}) custom-call(bf16[1024,512]{1,0:T(8,128)(2,1)S(1)} %copy-done.7, bf16[1024,512]{1,0:T(8,128)(2,1)S(1)} %copy-done.8, bf16[1024,512]{1,0:T(8,128)(2,1)S(1)} %copy-done.9, ...), custom_call_target="tpu_custom_call" | custom-call | tf_op jit(solution)/shard_map/backward_kernel/pallas_call | solution.py:558
  43.2 0.0 copy-done.1
  43.2 0.0 copy-done.4
  43.2 0.0 copy-done.5
  43.2 0.0 copy-start.6
  43.3 43.3 %total_kernel.1 = (bf16[3,2,4,4,64,128]{5,4,3,2,1,0:T(8,128)(2,1)S(1)}, bf16[3,2,4,4,64,128]{5,4,3,2,1,0:T(8,128)(2,1)S(1)}, bf16[1024,512]{1,0:T(8,128)(2,1)S(1...) custom-call(bf16[2,2,4,4,64,128]{5,4,3,2,1,0:T(8,128)(2,1)S(1)} %get-tuple-element.33.even_in, ...), custom_call_target="tpu_custom_call" | custom-call | tf_op jit(solution)/shard_map/total_kernel/pallas_call | solution.py:558
  86.6 0.0 copy-done.6
  86.6 3.4 %final_kernel.1 = (bf16[1024,512]{1,0:T(8,128)(2,1)}, bf16[1024,512]{1,0:T(8,128)(2,1)}, bf16[1024,512]{1,0:T(8,128)(2,1)}, f32[512,512]{1,0:T(8,128)}, f32[512,...) custom-call(bf16[1024,512]{1,0:T(8,128)(2,1)S(1)} %copy-done.1, bf16[1024,512]{1,0:T(8,128)(2,1)S(1)} %copy-done, ...), custom_call_target="tpu_custom_call" | custom-call | tf_op jit(solution)/shard_map/final_kernel/pallas_call | solution.py:558
Async XLA Ops:
  0.6 14.2 %copy-start = (bf16[1024,512]{1,0:T(8,128)(2,1)S(1)}, bf16[1024,512]{1,0:T(8,128)(2,1)}, u32[]{:S(2)}) copy-start(bf16[1024,512]{1,0:T(8,128)(2,1)} %grad_out.5) | copy-start | bytes 3145732
  0.6 14.2 %copy-start.2 = (bf16[512,512]{1,0:T(8,128)(2,1)S(1)}, bf16[512,512]{1,0:T(8,128)(2,1)}, u32[]{:S(2)}) copy-start(bf16[512,512]{1,0:T(8,128)(2,1)} %w_out.3) | copy-start | bytes 1572868
  0.7 0.8 copy-start.11
  1.5 13.4 %copy-start.3 = (bf16[1024,512]{1,0:T(8,128)(2,1)S(1)}, bf16[1024,512]{1,0:T(8,128)(2,1)}, u32[]{:S(2)}) copy-start(bf16[1024,512]{1,0:T(8,128)(2,1)} %hits.1) | copy-start | bytes 3145732
  14.8 19.7 %copy-start.7 = (bf16[1024,512]{1,0:T(8,128)(2,1)S(1)}, bf16[1024,512]{1,0:T(8,128)(2,1)}, u32[]{:S(2)}) copy-start(bf16[1024,512]{1,0:T(8,128)(2,1)} %get-tuple-element.25.q) | copy-start | bytes 3145732
  14.8 19.7 %copy-start.8 = (bf16[1024,512]{1,0:T(8,128)(2,1)S(1)}, bf16[1024,512]{1,0:T(8,128)(2,1)}, u32[]{:S(2)}) copy-start(bf16[1024,512]{1,0:T(8,128)(2,1)} %get-tuple-element.26.k) | copy-start | bytes 3145732
  14.8 19.7 %copy-start.10 = (bf16[2,4,4,64,128]{4,3,2,1,0:T(8,128)(2,1)S(1)}, bf16[2,4,4,64,128]{4,3,2,1,0:T(8,128)(2,1)}, u32[]{:S(2)}) copy-start(bf16[2,4,4,64,128]{4,3,2,1,0:T(8,128)(2,1)} %get-tuple-element.32.natt_o) | copy-start | bytes 1572868
  34.5 1.2 %copy-start.9 = (bf16[1024,512]{1,0:T(8,128)(2,1)S(1)}, bf16[1024,512]{1,0:T(8,128)(2,1)}, u32[]{:S(2)}) copy-start(bf16[1024,512]{1,0:T(8,128)(2,1)} %get-tuple-element.27.v) | copy-start | bytes 3145732
  35.7 7.5 %copy-start.1 = (bf16[1024,512]{1,0:T(8,128)(2,1)S(1)}, bf16[1024,512]{1,0:T(8,128)(2,1)}, u32[]{:S(2)}) copy-start(bf16[1024,512]{1,0:T(8,128)(2,1)} %queries.3) | copy-start | bytes 3145732
  35.7 7.5 %copy-start.4 = (bf16[512,512]{1,0:T(8,128)(2,1)S(1)}, bf16[512,512]{1,0:T(8,128)(2,1)}, u32[]{:S(2)}) copy-start(bf16[512,512]{1,0:T(8,128)(2,1)} %w_key.1) | copy-start | bytes 1572868
  35.7 7.5 %copy-start.5 = (bf16[512,512]{1,0:T(8,128)(2,1)S(1)}, bf16[512,512]{1,0:T(8,128)(2,1)}, u32[]{:S(2)}) copy-start(bf16[512,512]{1,0:T(8,128)(2,1)} %w_value.1) | copy-start | bytes 1572868
  43.2 43.3 %copy-start.6 = (bf16[512,512]{1,0:T(8,128)(2,1)S(1)}, bf16[512,512]{1,0:T(8,128)(2,1)}, u32[]{:S(2)}) copy-start(bf16[512,512]{1,0:T(8,128)(2,1)} %w_query.1) | copy-start | bytes 1572868

commit v4 on v3

--- a/solution.py
+++ b/solution.py
@@ -55,6 +55,24 @@
         counts[qb] = count
 
 
+def list_pairs(mask_ref, pairs):
+    first = lax.axis_index("region") * HB
+    slot = mask_ref[...] - first
+    inside = (slot >= 0) & (slot < HB)
+    weight = jnp.where(inside, jnp.left_shift(1, jnp.clip(slot, 0, HB - 1)), 0).astype(f32)
+    count = jnp.int32(0)
+    for qb in range(QB):
+        bits = jnp.sum(weight[qb : qb + 1, :]).astype(jnp.int32)
+        for hb in range(HB):
+            pairs[0, count] = qb
+            pairs[1, count] = hb
+            count = count + (jnp.right_shift(bits, hb) & 1)
+    for i in range(2):
+        pairs[0, count + i] = QB
+        pairs[1, count + i] = 0
+    return count
+
+
 def over_listed(lists, counts, qb, body):
     count = counts[qb]
 
@@ -99,21 +117,17 @@
 def forward_kernel(queries_h, hits_h, w_query_h, w_key_h, w_value_h, grad_out_h, w_out_h, mask_ref,
                    q_h, k_h, v_h, natt_e, natt_o, stats,
                    queries, hits, w_query, w_key, w_value, grad_out, w_out, q, k, v,
-                   gatt_t, heads_q, acc, peak, total, lists, counts, sems_in, sems_out):
+                   gatt_t, heads_q, acc, peak, total, scores_a, scores_b, pairs, sems_in, sems_out):
     ins = loads(
         ((hits_h, hits), (w_value_h, w_value), (w_key_h, w_key), (queries_h, queries),
          (w_query_h, w_query), (grad_out_h, grad_out), (w_out_h, w_out)), sems_in)
-    list_blocks(mask_ref, lists, counts)
     masks = lane_masks()
 
     def project(src, weight, out, scale=None):
-        def part(i, _):
-            rows = pl.ds(pl.multiple_of(i * 256, 256), 256)
+        for i in range(2):
+            rows = slice(i * 512, i * 512 + 512)
             x = dot(src[rows, :], weight[...])
             out[rows, :] = (x if scale is None else x * scale).astype(bf16)
-            return 0
-
-        lax.fori_loop(0, 4, part, 0)
 
     ins[0].wait()
     ins[1].wait()
@@ -127,50 +141,68 @@
     ins[4].wait()
     project(queries, w_query, q, SCALE)
     saves += loads(((q, q_h),), sems_out.at[pl.ds(2, 1)])
+    count = list_pairs(mask_ref, pairs)
     ins[5].wait()
     ins[6].wait()
 
-    def grads(i, _):
-        x = dot(w_out[...], grad_out[pl.ds(pl.multiple_of(i * 256, 256), 256), :], NT).astype(bf16)
+    for i in range(4):
+        x = dot(w_out[...], grad_out[i * 256 : i * 256 + 256, :], NT).astype(bf16)
         gatt_t[2 * i] = x[:, :B]
         gatt_t[2 * i + 1] = x[:, B:]
-        return 0
-
-    lax.fori_loop(0, 4, grads, 0)
-
-    def query_block(qb, _):
+
+    def spread(qb, _):
         rows = q[block_rows(qb), :]
         for p in range(PAIRS):
-            spread_heads(rows, p, heads_q, masks)
-        peak[...] = jnp.full(peak.shape, NEG, f32)
-        total[...] = jnp.zeros(total.shape, f32)
-        acc[...] = jnp.zeros(acc.shape, f32)
-
-        def body(blocks):
-            ps = range(PAIRS)
-            scores = [dot(gathered_rows(k, blocks, pair_cols(p)), heads_q[p], NT) for p in ps]
-            old = [peak[p] for p in ps]
-            new = [jnp.maximum(o, jnp.max(s, axis=0, keepdims=True)) for o, s in zip(old, scores)]
-            shrink = [jnp.exp(o - n) for o, n in zip(old, new)]
-            expo = [jnp.exp(s - n) for s, n in zip(scores, new)]
-            numer = [dot(gathered_rows(v, blocks, pair_cols(p)), expo[p].astype(bf16), TN) for p in ps]
-            for p in ps:
-                peak[p] = new[p]
-                total[p] = total[p] * shrink[p] + jnp.sum(expo[p], axis=0, keepdims=True)
-                acc[p, :64] = acc[p, :64] * shrink[p][:, :B] + numer[p][:64, :B]
-                acc[p, 64:] = acc[p, 64:] * shrink[p][:, B:] + numer[p][64:, B:]
-
-        over_listed(lists, counts, qb, body)
+            spread_heads(rows, p, heads_q.at[qb], masks)
+        return 0
+
+    lax.fori_loop(0, QB, spread, 0)
+    heads_q[QB] = jnp.zeros(heads_q.shape[1:], bf16)
+    peak[...] = jnp.full(peak.shape, NEG, f32)
+    total[...] = jnp.zeros(total.shape, f32)
+    acc[...] = jnp.zeros(acc.shape, f32)
+    ps = range(PAIRS)
+
+    def score(i, out):
+        qb, hb = pairs[0, i], pairs[1, i]
+        for p in ps:
+            out[p] = dot(k[block_rows(hb), pair_cols(p)], heads_q[qb, p], NT)
+
+    def add(i, scores):
+        qb, hb = pairs[0, i], pairs[1, i]
+        old = [peak[qb, p] for p in ps]
+        new = [jnp.maximum(old[p], jnp.max(scores[p], axis=0, keepdims=True)) for p in ps]
+        shrink = [jnp.exp(old[p] - new[p]) for p in ps]
+        expo = [jnp.exp(scores[p] - new[p]) for p in ps]
+        numer = [dot(v[block_rows(hb), pair_cols(p)], expo[p].astype(bf16), TN) for p in ps]
+        for p in ps:
+            peak[qb, p] = new[p]
+            total[qb, p] = total[qb, p] * shrink[p] + jnp.sum(expo[p], axis=0, keepdims=True)
+            acc[qb, p, :64] = acc[qb, p, :64] * shrink[p][:, :B] + numer[p][:64, :B]
+            acc[qb, p, 64:] = acc[qb, p, 64:] * shrink[p][:, B:] + numer[p][64:, B:]
+
+    score(0, scores_a)
+
+    def two(j, _):
+        score(2 * j + 1, scores_b)
+        add(2 * j, scores_a)
+        score(2 * j + 2, scores_a)
+        add(2 * j + 1, scores_b)
+        return 0
+
+    lax.fori_loop(0, (count + 1) // 2, two, 0)
+
+    def query_block(qb, _):
         core, z = qb // 4, lax.rem(qb, 4)
         for p in range(PAIRS):
-            some = total[p] > 0.0
-            safe = jnp.where(some, total[p], 1.0)
-            log_total = jnp.where(some, peak[p] + jnp.log(safe), NEG)
+            some = total[qb, p] > 0.0
+            safe = jnp.where(some, total[qb, p], 1.0)
+            log_total = jnp.where(some, peak[qb, p] + jnp.log(safe), NEG)
             inverse = 1.0 / safe
             for half, out in enumerate((natt_e.at[core, p, z], natt_o.at[core, z, p])):
                 lanes = slice(half * B, (half + 1) * B)
                 rows = slice(half * 64, half * 64 + 64)
-                part = acc[p, rows] * inverse[:, lanes]
+                part = acc[qb, p, rows] * inverse[:, lanes]
                 out[...] = part.astype(bf16)
                 grads = gatt_t[qb, p * B + half * 64 : p * B + half * 64 + 64, :].astype(f32)
                 h = 2 * p + half
@@ -485,10 +517,10 @@
             got(gath.at[1 - core, own], f + 3)
 
     for step, c in (
-        (send_pair, 0), (send_pair, 1), (add_cores, 0), (add_cores, 1), (weight_grads, 2), (add_first, 0),
-        (add_first, 1), (add_cores, 2), (hit_grads, 0), (add_second, 0), (add_second, 1), (hit_grads, 1),
-        (add_first, 2), (pass_row, 0), (pass_row, 1), (add_second, 2), (pass_sibling, 0), (pass_sibling, 1),
-        (pass_row, 2), (from_sibling, 0), (attended_products, 0), (pass_sibling, 2), (from_sibling, 1),
+        (send_pair, 0), (send_pair, 1), (add_cores, 0), (weight_grads, 2), (add_cores, 1), (add_first, 0),
+        (add_cores, 2), (add_first, 1), (hit_grads, 0), (add_second, 0), (add_first, 2), (add_second, 1),
+        (hit_grads, 1), (pass_row, 0), (add_second, 2), (pass_row, 1), (pass_sibling, 0), (pass_row, 2),
+        (pass_sibling, 1), (from_sibling, 0), (attended_products, 0), (pass_sibling, 2), (from_sibling, 1),
         (from_sibling, 2),
     ):
         step(c)
@@ -551,7 +583,7 @@
     return pltpu.VMEM(shape, dtype)
 
 
-def call(kernel, args, outs, scratch_shapes, collective=None, any_in=(), any_out=(), vmem=VMEM_LIMIT):
+def call(kernel, args, outs, scratch_shapes, collective=None, any_in=(), any_out=(), vmem=VMEM_LIMIT, flops=None):
     params = {"vmem_limit_bytes": vmem}
     if collective is not None:
         params |= {"collective_id": collective, "has_side_effects": True}
@@ -562,6 +594,7 @@
         out_specs=tuple(ANY if i in any_out else VMEM for i in range(len(outs))),
         scratch_shapes=scratch_shapes,
         compiler_params=pltpu.CompilerParams(**params),
+        cost_estimate=flops and pl.CostEstimate(flops=flops, bytes_accessed=4 * MIB, transcendentals=0),
         name=kernel.__name__,
     )(*args)
 
@@ -583,9 +616,11 @@
         ),
         [
             full, full, weight, weight, weight, full, weight, full, full, full,
-            turned, spread, scratch(PAIRS, B, B, dtype=f32),
-            scratch(PAIRS, 1, 2 * B, dtype=f32), scratch(PAIRS, 1, 2 * B, dtype=f32),
-        ] + lists + [DMA((7,)), DMA((3,))],
+            turned, scratch(QB + 1, PAIRS, 2 * B, B), scratch(QB + 1, PAIRS, B, B, dtype=f32),
+            scratch(QB + 1, PAIRS, 1, 2 * B, dtype=f32), scratch(QB + 1, PAIRS, 1, 2 * B, dtype=f32),
+            scratch(PAIRS, B, 2 * B, dtype=f32), scratch(PAIRS, B, 2 * B, dtype=f32),
+            pltpu.SMEM((2, QB * HB + 2), jnp.int32), DMA((7,)), DMA((3,)),
+        ],
         any_in=range(7),
         any_out=range(3),
         vmem=FORWARD_LIMIT,
@@ -605,6 +640,7 @@
         ],
         collective=0,
         vmem=8 * MIB,
+        flops=2 * 10**10,
     )
     even, odd, dkb, dvb = call(
         backward_kernel,

time: 90.2 us -> 77.5 us (0.86)
  Pallas kernels: 87.1 us -> 75.7 us
  local copies, waits for them, and re-layouts: 2.06 us -> 0.86 us
    pallas_call x5, Pallas kernels: 87.1 us -> 75.7 us  [call(): pl.pallas_call(kernel, out_shape=outs, in_specs=[ANY if i in any_in else...]
    unnamed x24, local copies, waits for them, and re-layouts: 2.06 us -> 0.86 us
where the time goes in v4:
time: 77.5 us; the launch traced here: 77.4 us
  Pallas kernels  75.7 us (98%)
  local copies, waits for them, and re-layouts  0.86 us (1%)
  between operations  0.84 us (1%)
    pallas_call x5, Pallas kernels, call(): pl.pallas_call(kernel, out_shape=outs, in_specs=[ANY if i in any_in else...  75.7 us

profile of v4, /device:TPU:1, one launch (start us, length us, event | category | flops | bytes accessed | tf_op | source)
XLA Modules:
  0.0 77.4 jit_solution(16036707281340946089)
XLA Ops:
  0.6 0.0 copy-start.1
  0.6 0.0 copy-start.4
  0.7 0.0 copy-start.11
  0.7 0.8 %copy-done.11 = s32[8,64]{1,0:T(8,128)S(1)} copy-done((s32[8,64]{1,0:T(8,128)S(1)}, s32[8,64]{1,0:T(8,128)}, u32[]{:S(2)}) %copy-start.11) | copy-done | bytes 2072
  1.5 0.0 copy-start.6
  1.5 11.2 %forward_kernel.1 = (bf16[1024,512]{1,0:T(8,128)(2,1)}, bf16[1024,512]{1,0:T(8,128)(2,1)}, bf16[1024,512]{1,0:T(8,128)(2,1)}, bf16[2,4,4,64,128]{4,3,2,1,0:T(8,1...) custom-call(bf16[1024,512]{1,0:T(8,128)(2,1)} %queries.3, bf16[1024,512]{1,0:T(8,128)(2,1)} %hits.1, ...), custom_call_target="tpu_custom_call" | custom-call | tf_op jit(solution)/shard_map/forward_kernel/pallas_call | solution.py:590
  12.6 0.0 copy-done.1
  12.7 0.0 copy-done.4
  12.7 0.0 copy-done.6
  12.7 0.0 copy-start.7
  12.7 0.0 copy-start.8
  12.7 0.0 copy-start.9
  12.7 0.0 copy-start.10
  12.7 16.4 %softmax_kernel.1 = (f32[8,16,128]{2,1,0:T(8,128)S(1)}, bf16[8,512,128]{2,1,0:T(8,128)(2,1)S(1)}, bf16[1024,512]{1,0:T(8,128)(2,1)S(1)}) custom-call(f32[8,16,128]{2,1,0:T(8,128)S(1)} %get-tuple-element.28.stats_in.stats_own, bf16[1024,512]{1,0:T(8,128)(2,1)S(1)} %copy-done.6, bf16[1024,512]{1,0:T(8,128)(2,1)S(1)} %copy-done.1, bf16[512,512]{1,0:T(8,128)(2,1)S(1)} %copy-done.4), custom_call_target="tpu_custom_call" | custom-call | flops 20000000000 | bytes 4194304 | tf_op jit(solution)/shard_map/softmax_kernel/pallas_call | solution.py:590
  29.1 0.0 copy-done.7
  29.1 0.0 copy-done.8
  29.1 0.0 copy-done.9
  29.1 0.0 copy-done.10
  29.2 0.0 copy-start
  29.2 0.0 copy-start.2
  29.2 0.0 copy-start.3
  29.2 9.4 %backward_kernel.1 = (bf16[2,2,4,4,64,128]{5,4,3,2,1,0:T(8,128)(2,1)S(1)}, bf16[2,2,4,4,64,128]{5,4,3,2,1,0:T(8,128)(2,1)S(1)}, bf16[1024,512]{1,0:T(8,128)(2,1)S(1)}, bf16[1024,512]{1,0:T(8,128)(2,1)S(1)}) custom-call(bf16[1024,512]{1,0:T(8,128)(2,1)S(1)} %copy-done.7, bf16[1024,512]{1,0:T(8,128)(2,1)S(1)} %copy-done.8, bf16[1024,512]{1,0:T(8,128)(2,1)S(1)} %copy-done.9, ...), custom_call_target="tpu_custom_call" | custom-call | tf_op jit(solution)/shard_map/backward_kernel/pallas_call | solution.py:590
  38.6 0.0 copy-done
  38.6 0.0 copy-done.2
  38.6 0.0 copy-done.3
  38.6 0.0 copy-start.5
  38.6 35.3 %total_kernel.1 = (bf16[3,2,4,4,64,128]{5,4,3,2,1,0:T(8,128)(2,1)S(1)}, bf16[3,2,4,4,64,128]{5,4,3,2,1,0:T(8,128)(2,1)S(1)}, bf16[1024,512]{1,0:T(8,128)(2,1)S(1...) custom-call(bf16[2,2,4,4,64,128]{5,4,3,2,1,0:T(8,128)(2,1)S(1)} %get-tuple-element.33.even_in, ...), custom_call_target="tpu_custom_call" | custom-call | tf_op jit(solution)/shard_map/total_kernel/pallas_call | solution.py:590
  73.9 0.0 copy-done.5
  74.0 3.4 %final_kernel.1 = (bf16[1024,512]{1,0:T(8,128)(2,1)}, bf16[1024,512]{1,0:T(8,128)(2,1)}, bf16[1024,512]{1,0:T(8,128)(2,1)}, f32[512,512]{1,0:T(8,128)}, f32[512,...) custom-call(bf16[1024,512]{1,0:T(8,128)(2,1)S(1)} %copy-done, bf16[1024,512]{1,0:T(8,128)(2,1)S(1)} %copy-done.1, ...), custom_call_target="tpu_custom_call" | custom-call | tf_op jit(solution)/shard_map/final_kernel/pallas_call | solution.py:590
Async XLA Ops:
  0.6 12.0 %copy-start.1 = (bf16[1024,512]{1,0:T(8,128)(2,1)S(1)}, bf16[1024,512]{1,0:T(8,128)(2,1)}, u32[]{:S(2)}) copy-start(bf16[1024,512]{1,0:T(8,128)(2,1)} %grad_out.5) | copy-start | bytes 3145732
  0.6 12.0 %copy-start.4 = (bf16[512,512]{1,0:T(8,128)(2,1)S(1)}, bf16[512,512]{1,0:T(8,128)(2,1)}, u32[]{:S(2)}) copy-start(bf16[512,512]{1,0:T(8,128)(2,1)} %w_out.3) | copy-start | bytes 1572868
  0.7 0.8 %copy-start.11 = (s32[8,64]{1,0:T(8,128)S(1)}, s32[8,64]{1,0:T(8,128)}, u32[]{:S(2)}) copy-start(s32[8,64]{1,0:T(8,128)} %mask_ref.3) | copy-start | bytes 6148
  1.5 11.2 %copy-start.6 = (bf16[1024,512]{1,0:T(8,128)(2,1)S(1)}, bf16[1024,512]{1,0:T(8,128)(2,1)}, u32[]{:S(2)}) copy-start(bf16[1024,512]{1,0:T(8,128)(2,1)} %hits.1) | copy-start | bytes 3145732
  12.7 16.5 %copy-start.7 = (bf16[1024,512]{1,0:T(8,128)(2,1)S(1)}, bf16[1024,512]{1,0:T(8,128)(2,1)}, u32[]{:S(2)}) copy-start(bf16[1024,512]{1,0:T(8,128)(2,1)} %get-tuple-element.25.q) | copy-start | bytes 3145732
  12.7 16.4 %copy-start.8 = (bf16[1024,512]{1,0:T(8,128)(2,1)S(1)}, bf16[1024,512]{1,0:T(8,128)(2,1)}, u32[]{:S(2)}) copy-start(bf16[1024,512]{1,0:T(8,128)(2,1)} %get-tuple-element.26.k) | copy-start | bytes 3145732
  12.7 16.4 %copy-start.9 = (bf16[1024,512]{1,0:T(8,128)(2,1)S(1)}, bf16[1024,512]{1,0:T(8,128)(2,1)}, u32[]{:S(2)}) copy-start(bf16[1024,512]{1,0:T(8,128)(2,1)} %get-tuple-element.27.v) | copy-start | bytes 3145732
  12.7 16.4 %copy-start.10 = (bf16[2,4,4,64,128]{4,3,2,1,0:T(8,128)(2,1)S(1)}, bf16[2,4,4,64,128]{4,3,2,1,0:T(8,128)(2,1)}, u32[]{:S(2)}) copy-start(bf16[2,4,4,64,128]{4,3,2,1,0:T(8,128)(2,1)} %get-tuple-element.32.natt_o) | copy-start | bytes 1572868
  29.2 9.4 %copy-start = (bf16[1024,512]{1,0:T(8,128)(2,1)S(1)}, bf16[1024,512]{1,0:T(8,128)(2,1)}, u32[]{:S(2)}) copy-start(bf16[1024,512]{1,0:T(8,128)(2,1)} %queries.3) | copy-start | bytes 3145732
  29.2 9.4 %copy-start.2 = (bf16[512,512]{1,0:T(8,128)(2,1)S(1)}, bf16[512,512]{1,0:T(8,128)(2,1)}, u32[]{:S(2)}) copy-start(bf16[512,512]{1,0:T(8,128)(2,1)} %w_key.1) | copy-start | bytes 1572868
  29.2 9.4 %copy-start.3 = (bf16[512,512]{1,0:T(8,128)(2,1)S(1)}, bf16[512,512]{1,0:T(8,128)(2,1)}, u32[]{:S(2)}) copy-start(bf16[512,512]{1,0:T(8,128)(2,1)} %w_value.1) | copy-start | bytes 1572868
  38.6 35.3 %copy-start.5 = (bf16[512,512]{1,0:T(8,128)(2,1)S(1)}, bf16[512,512]{1,0:T(8,128)(2,1)}, u32[]{:S(2)}) copy-start(bf16[512,512]{1,0:T(8,128)(2,1)} %w_query.1) | copy-start | bytes 1572868

commit v5 on v4

--- a/solution.py
+++ b/solution.py
@@ -347,17 +347,16 @@
             h = base + 2 * p
             return jnp.concatenate([stats[qb, h : h + 1, :], stats[qb, h + 1 : h + 2, :]], axis=1)
 
-        def body(blocks):
-            ps = range(PAIRS)
-            keys = [gathered_rows(k, blocks, pair_cols(p)) for p in ps]
-            vals = [gathered_rows(v, blocks, pair_cols(p)) for p in ps]
-            scores = [dot(keys[p], heads_q[p], NT) for p in ps]
-            dps = [dot(vals[p], heads_g[p], NT) for p in ps]
-            probs = [jnp.exp(scores[p] - stat_row(p, 0)) for p in ps]
-            ds = [(probs[p] * (dps[p] - stat_row(p, 8))).astype(bf16) for p in ps]
-            dvs = [dot(probs[p].astype(bf16), heads_g[p]) for p in ps]
-            dks = [dot(ds[p], heads_q[p]) for p in ps]
-            dqs = [dot(keys[p], ds[p], TN) for p in ps]
+        def some_heads(blocks, ps):
+            keys = {p: gathered_rows(k, blocks, pair_cols(p)) for p in ps}
+            vals = {p: gathered_rows(v, blocks, pair_cols(p)) for p in ps}
+            scores = {p: dot(keys[p], heads_q[p], NT) for p in ps}
+            dps = {p: dot(vals[p], heads_g[p], NT) for p in ps}
+            probs = {p: jnp.exp(scores[p] - stat_row(p, 0)) for p in ps}
+            ds = {p: (probs[p] * (dps[p] - stat_row(p, 8))).astype(bf16) for p in ps}
+            dvs = {p: dot(probs[p].astype(bf16), heads_g[p]) for p in ps}
+            dks = {p: dot(ds[p], heads_q[p]) for p in ps}
+            dqs = {p: dot(keys[p], ds[p], TN) for p in ps}
             for p in ps:
                 for j, b in enumerate(blocks):
                     part = slice(j * B, (j + 1) * B)
@@ -365,6 +364,11 @@
                     dk[block_rows(b), pair_cols(p)] += dks[p][part]
                 acc[p, :64] = acc[p, :64] + dqs[p][:64, :B]
                 acc[p, 64:] = acc[p, 64:] + dqs[p][64:, B:]
+
+        def body(blocks):
+            at_once = PAIRS // len(blocks)
+            for p in range(0, PAIRS, at_once):
+                some_heads(blocks, range(p, p + at_once))
 
         over_listed(lists, counts, qb, body)
         for p in range(PAIRS):
@@ -517,7 +521,7 @@
             got(gath.at[1 - core, own], f + 3)
 
     for step, c in (
-        (send_pair, 0), (send_pair, 1), (add_cores, 0), (weight_grads, 2), (add_cores, 1), (add_first, 0),
+        (send_pair, 0), (send_pair, 1), (add_cores, 0), (add_cores, 1), (weight_grads, 2), (add_first, 0),
         (add_cores, 2), (add_first, 1), (hit_grads, 0), (add_second, 0), (add_first, 2), (add_second, 1),
         (hit_grads, 1), (pass_row, 0), (add_second, 2), (pass_row, 1), (pass_sibling, 0), (pass_row, 2),
         (pass_sibling, 1), (from_sibling, 0), (attended_products, 0), (pass_sibling, 2), (from_sibling, 1),

time: 77.5 us -> 77.8 us (level)
  Pallas kernels: 75.7 us -> 76.5 us
    pallas_call x5, Pallas kernels: 75.7 us -> 76.5 us  [call(): pl.pallas_call(kernel, out_shape=outs, in_specs=[ANY if i in any_in else...]
where the time goes in v5:
time: 77.8 us; the launch traced here: 78.2 us
  Pallas kernels  76.5 us (98%)
  local copies, waits for them, and re-layouts  0.86 us (1%)
  between operations  0.84 us (1%)
    pallas_call x5, Pallas kernels, call(): pl.pallas_call(kernel, out_shape=outs, in_specs=[ANY if i in any_in else...  76.5 us

profile of v5, /device:TPU:1, one launch (start us, length us, event | category | flops | bytes accessed | tf_op | source)
XLA Modules:
  0.0 78.2 jit_solution(2425707625903766043)
XLA Ops:
  0.6 0.0 copy-start.1
  0.6 0.0 copy-start.4
  0.7 0.0 copy-start.11
  0.7 0.8 %copy-done.11 = s32[8,64]{1,0:T(8,128)S(1)} copy-done((s32[8,64]{1,0:T(8,128)S(1)}, s32[8,64]{1,0:T(8,128)}, u32[]{:S(2)}) %copy-start.11) | copy-done | bytes 2072
  1.5 0.0 copy-start.6
  1.5 9.6 %forward_kernel.1 = (bf16[1024,512]{1,0:T(8,128)(2,1)}, bf16[1024,512]{1,0:T(8,128)(2,1)}, bf16[1024,512]{1,0:T(8,128)(2,1)}, bf16[2,4,4,64,128]{4,3,2,1,0:T(8,1...) custom-call(bf16[1024,512]{1,0:T(8,128)(2,1)} %queries.3, bf16[1024,512]{1,0:T(8,128)(2,1)} %hits.1, ...), custom_call_target="tpu_custom_call" | custom-call | tf_op jit(solution)/shard_map/forward_kernel/pallas_call | solution.py:594
  11.1 0.0 copy-done.1
  11.1 0.0 copy-done.4
  11.1 0.0 copy-done.6
  11.1 0.0 copy-start.7
  11.1 0.0 copy-start.8
  11.1 0.0 copy-start.9
  11.1 0.0 copy-start.10
  11.1 19.4 %softmax_kernel.1 = (f32[8,16,128]{2,1,0:T(8,128)S(1)}, bf16[8,512,128]{2,1,0:T(8,128)(2,1)S(1)}, bf16[1024,512]{1,0:T(8,128)(2,1)S(1)}) custom-call(f32[8,16,128]{2,1,0:T(8,128)S(1)} %get-tuple-element.28.stats_in.stats_own, bf16[1024,512]{1,0:T(8,128)(2,1)S(1)} %copy-done.6, bf16[1024,512]{1,0:T(8,128)(2,1)S(1)} %copy-done.1, bf16[512,512]{1,0:T(8,128)(2,1)S(1)} %copy-done.4), custom_call_target="tpu_custom_call" | custom-call | flops 20000000000 | bytes 4194304 | tf_op jit(solution)/shard_map/softmax_kernel/pallas_call | solution.py:594
  30.6 0.0 copy-done.7
  30.6 0.0 copy-done.8
  30.6 0.0 copy-done.9
  30.6 0.0 copy-done.10
  30.6 0.0 copy-start
  30.6 0.0 copy-start.2
  30.6 0.0 copy-start.3
  30.6 6.4 %backward_kernel.1 = (bf16[2,2,4,4,64,128]{5,4,3,2,1,0:T(8,128)(2,1)S(1)}, bf16[2,2,4,4,64,128]{5,4,3,2,1,0:T(8,128)(2,1)S(1)}, bf16[1024,512]{1,0:T(8,128)(2,1)S(1)}, bf16[1024,512]{1,0:T(8,128)(2,1)S(1)}) custom-call(bf16[1024,512]{1,0:T(8,128)(2,1)S(1)} %copy-done.7, bf16[1024,512]{1,0:T(8,128)(2,1)S(1)} %copy-done.8, bf16[1024,512]{1,0:T(8,128)(2,1)S(1)} %copy-done.9, ...), custom_call_target="tpu_custom_call" | custom-call | tf_op jit(solution)/shard_map/backward_kernel/pallas_call | solution.py:594
  37.1 0.0 copy-done
  37.1 0.0 copy-done.2
  37.1 0.0 copy-done.3
  37.1 0.0 copy-start.5
  37.1 37.6 %total_kernel.1 = (bf16[3,2,4,4,64,128]{5,4,3,2,1,0:T(8,128)(2,1)S(1)}, bf16[3,2,4,4,64,128]{5,4,3,2,1,0:T(8,128)(2,1)S(1)}, bf16[1024,512]{1,0:T(8,128)(2,1)S(1...) custom-call(bf16[2,2,4,4,64,128]{5,4,3,2,1,0:T(8,128)(2,1)S(1)} %get-tuple-element.33.even_in, ...), custom_call_target="tpu_custom_call" | custom-call | tf_op jit(solution)/shard_map/total_kernel/pallas_call | solution.py:594
  74.7 0.0 copy-done.5
  74.8 3.4 %final_kernel.1 = (bf16[1024,512]{1,0:T(8,128)(2,1)}, bf16[1024,512]{1,0:T(8,128)(2,1)}, bf16[1024,512]{1,0:T(8,128)(2,1)}, f32[512,512]{1,0:T(8,128)}, f32[512,...) custom-call(bf16[1024,512]{1,0:T(8,128)(2,1)S(1)} %copy-done, bf16[1024,512]{1,0:T(8,128)(2,1)S(1)} %copy-done.1, ...), custom_call_target="tpu_custom_call" | custom-call | tf_op jit(solution)/shard_map/final_kernel/pallas_call | solution.py:594
Async XLA Ops:
  0.6 10.4 %copy-start.1 = (bf16[1024,512]{1,0:T(8,128)(2,1)S(1)}, bf16[1024,512]{1,0:T(8,128)(2,1)}, u32[]{:S(2)}) copy-start(bf16[1024,512]{1,0:T(8,128)(2,1)} %grad_out.5) | copy-start | bytes 3145732
  0.6 10.4 %copy-start.4 = (bf16[512,512]{1,0:T(8,128)(2,1)S(1)}, bf16[512,512]{1,0:T(8,128)(2,1)}, u32[]{:S(2)}) copy-start(bf16[512,512]{1,0:T(8,128)(2,1)} %w_out.3) | copy-start | bytes 1572868
  0.7 0.8 %copy-start.11 = (s32[8,64]{1,0:T(8,128)S(1)}, s32[8,64]{1,0:T(8,128)}, u32[]{:S(2)}) copy-start(s32[8,64]{1,0:T(8,128)} %mask_ref.3) | copy-start | bytes 6148
  1.5 9.6 %copy-start.6 = (bf16[1024,512]{1,0:T(8,128)(2,1)S(1)}, bf16[1024,512]{1,0:T(8,128)(2,1)}, u32[]{:S(2)}) copy-start(bf16[1024,512]{1,0:T(8,128)(2,1)} %hits.1) | copy-start | bytes 3145732
  11.1 19.5 %copy-start.7 = (bf16[1024,512]{1,0:T(8,128)(2,1)S(1)}, bf16[1024,512]{1,0:T(8,128)(2,1)}, u32[]{:S(2)}) copy-start(bf16[1024,512]{1,0:T(8,128)(2,1)} %get-tuple-element.25.q) | copy-start | bytes 3145732
  11.1 19.5 %copy-start.8 = (bf16[1024,512]{1,0:T(8,128)(2,1)S(1)}, bf16[1024,512]{1,0:T(8,128)(2,1)}, u32[]{:S(2)}) copy-start(bf16[1024,512]{1,0:T(8,128)(2,1)} %get-tuple-element.26.k) | copy-start | bytes 3145732
  11.1 19.5 %copy-start.9 = (bf16[1024,512]{1,0:T(8,128)(2,1)S(1)}, bf16[1024,512]{1,0:T(8,128)(2,1)}, u32[]{:S(2)}) copy-start(bf16[1024,512]{1,0:T(8,128)(2,1)} %get-tuple-element.27.v) | copy-start | bytes 3145732
  11.1 19.5 %copy-start.10 = (bf16[2,4,4,64,128]{4,3,2,1,0:T(8,128)(2,1)S(1)}, bf16[2,4,4,64,128]{4,3,2,1,0:T(8,128)(2,1)}, u32[]{:S(2)}) copy-start(bf16[2,4,4,64,128]{4,3,2,1,0:T(8,128)(2,1)} %get-tuple-element.32.natt_o) | copy-start | bytes 1572868
  30.6 6.5 %copy-start = (bf16[1024,512]{1,0:T(8,128)(2,1)S(1)}, bf16[1024,512]{1,0:T(8,128)(2,1)}, u32[]{:S(2)}) copy-start(bf16[1024,512]{1,0:T(8,128)(2,1)} %queries.3) | copy-start | bytes 3145732
  30.6 6.5 %copy-start.2 = (bf16[512,512]{1,0:T(8,128)(2,1)S(1)}, bf16[512,512]{1,0:T(8,128)(2,1)}, u32[]{:S(2)}) copy-start(bf16[512,512]{1,0:T(8,128)(2,1)} %w_key.1) | copy-start | bytes 1572868
  30.6 6.5 %copy-start.3 = (bf16[512,512]{1,0:T(8,128)(2,1)S(1)}, bf16[512,512]{1,0:T(8,128)(2,1)}, u32[]{:S(2)}) copy-start(bf16[512,512]{1,0:T(8,128)(2,1)} %w_value.1) | copy-start | bytes 1572868
  37.1 37.6 %copy-start.5 = (bf16[512,512]{1,0:T(8,128)(2,1)S(1)}, bf16[512,512]{1,0:T(8,128)(2,1)}, u32[]{:S(2)}) copy-start(bf16[512,512]{1,0:T(8,128)(2,1)} %w_query.1) | copy-start | bytes 1572868
